TPU v7x, 512 devices: a whole 4x8x8 slice. The times are simulated.
512 devices in a mesh: nodes: 256 (over z, y, x), heads: 2 (over core).
Axes of the slice: x: 4, y: 8, z: 8, core: 2. Of those that a mesh axis runs over, the one named last changes fastest.
Arguments:
- grid_fields: bfloat16 [100, 131072], P(None, ('nodes', 'heads')), may hold values from -6 to 6
- mesh_state: bfloat16 [32768, 1024], P('nodes'), may hold values from -6 to 6
- w_embed: bfloat16 [100, 1024], replicated, may hold values from -0.625 to 0.625
- w_query_enc: bfloat16 [1024, 1024], P(None, 'heads'), may hold values from -0.1875 to 0.1875
- w_key_enc: bfloat16 [1024, 1024], P(None, 'heads'), may hold values from -0.1875 to 0.1875
- w_value_enc: bfloat16 [1024, 1024], P(None, 'heads'), may hold values from -0.1875 to 0.1875
- w_out_enc: bfloat16 [1024, 1024], P('heads'), may hold values from -0.1875 to 0.1875
- w_query_proc: bfloat16 [1024, 1024], P(None, 'heads'), may hold values from -0.1875 to 0.1875
- w_key_proc: bfloat16 [1024, 1024], P(None, 'heads'), may hold values from -0.1875 to 0.1875
- w_value_proc: bfloat16 [1024, 1024], P(None, 'heads'), may hold values from -0.1875 to 0.1875
- w_out_proc: bfloat16 [1024, 1024], P('heads'), may hold values from -0.1875 to 0.1875
- send_rows: int32 [256, 4, 32], P('nodes'), may hold values from 0 to 511
- edge_senders: int32 [32768, 32], P('nodes'), may hold values from 0 to 639, as said below
- edge_mask: int32 [32768, 32], P('nodes'), may hold values from 0 to 1, as said below
Outputs:
- layer_out: bfloat16 [32768, 1024], P(('nodes', 'heads'))
Inputs may be any that keep to these rules, and one draw needn't show every extreme that they name: `edge_senders`: about three quarters of the edge slots point into the own region's rows, the rest into the neighbours' listed rows. `edge_mask`: the live edge slots of each mesh node come first, and every mesh node has at least one.
All inputs are finite; a program needn't handle non-finite values.
Results may differ from a plain program's by a relative error of at most 0.012.
Values may be sent and summed in bfloat16 or wider, within the bound.
A program may use at most 128 MiB of HBM per device.

v0:
```python
import math

import jax
import jax.numpy as jnp
from jax import lax
from jax.sharding import PartitionSpec as P

HEADS = 16
HS = 64
NEIGH = 4


def passed_along(block, axis, distance):
    devices = range(lax.axis_size(axis))
    route = [((i - distance) % len(devices), i) for i in devices]
    return lax.ppermute(block, axis, route)


def normalize(values):
    values = values.astype(jnp.float32)
    centred = values - jnp.mean(values, axis=-1, keepdims=True)
    spread = jnp.mean(centred * centred, axis=-1, keepdims=True)
    return centred * lax.rsqrt(spread + 1e-05)


def neighbour_offset(slot):
    return (slot // 2 + 1) * (1 if slot % 2 == 0 else -1)


def local(
    grid_fields,
    mesh_state,
    w_embed,
    w_query_enc,
    w_key_enc,
    w_value_enc,
    w_out_enc,
    w_query_proc,
    w_key_proc,
    w_value_proc,
    w_out_proc,
    send_rows,
    edge_senders,
    edge_mask,
):
    head_groups = lax.axis_size("heads")
    local_heads = HEADS // head_groups
    head_cols = local_heads * HS
    mesh_len = mesh_state.shape[0]
    own_rows = mesh_len // head_groups
    fan_slots = edge_senders.shape[1]
    logit_scale_factor = 1.0 / math.sqrt(HS)
    projected = lax.dot_general(
        grid_fields, w_embed, (((0,), (0,)), ((), ())), preferred_element_type=jnp.float32
    )
    embedded = normalize(projected).astype(jnp.bfloat16)

    def project(shard_rows, offset=0):
        keys_part = jnp.dot(shard_rows, w_key_enc, preferred_element_type=jnp.float32).astype(
            jnp.bfloat16
        )
        values_part = jnp.dot(shard_rows, w_value_enc, preferred_element_type=jnp.float32).astype(
            jnp.bfloat16
        )
        return jnp.concatenate([keys_part, values_part], axis=-1)

    listed_rows = send_rows[0]
    received = []
    region = lax.all_gather(embedded, "heads", axis=0, tiled=True)
    for slot in range(NEIGH):
        outgoing = region[listed_rows[slot]]
        received.append(passed_along(outgoing, "nodes", neighbour_offset(slot)))
    kv_table = project(jnp.concatenate([region] + received, axis=0))
    queries = jnp.dot(
        normalize(mesh_state).astype(jnp.bfloat16), w_query_enc, preferred_element_type=jnp.float32
    ).astype(jnp.bfloat16)
    queries = queries.reshape(mesh_len, local_heads, HS)
    picked = kv_table[edge_senders]
    keys_edge = picked[:, :, :head_cols].reshape(mesh_len, fan_slots, local_heads, HS)
    values_edge = picked[:, :, head_cols:].reshape(mesh_len, fan_slots, local_heads, HS)
    scores = (
        jnp.einsum("nhd,nfhd->nhf", queries, keys_edge, preferred_element_type=jnp.float32)
        * logit_scale_factor
    )
    weights = jnp.where(edge_mask[:, None, :] > 0, jnp.exp(scores), jnp.float32(0.0))
    enc_probs = (weights / jnp.sum(weights, axis=-1, keepdims=True)).astype(jnp.bfloat16)
    enc_context = jnp.einsum(
        "nhf,nfhd->nhd", enc_probs, values_edge, preferred_element_type=jnp.float32
    ).astype(jnp.bfloat16)
    enc_context = enc_context.reshape(mesh_len, head_cols)
    head_index = lax.axis_index("heads")

    def qkv_rows(shard_rows, offset=0):
        query_part = jnp.dot(shard_rows, w_query_proc, preferred_element_type=jnp.float32).astype(
            jnp.bfloat16
        )
        key_part = jnp.dot(shard_rows, w_key_proc, preferred_element_type=jnp.float32).astype(
            jnp.bfloat16
        )
        value_part = jnp.dot(shard_rows, w_value_proc, preferred_element_type=jnp.float32).astype(
            jnp.bfloat16
        )
        return jnp.concatenate([query_part, key_part, value_part], axis=-1)

    encoder_rows = lax.psum_scatter(
        jnp.dot(enc_context, w_out_enc, preferred_element_type=jnp.float32).astype(jnp.bfloat16),
        "heads",
        scatter_dimension=0,
        tiled=True,
    ).astype(jnp.float32)
    own_state = lax.dynamic_slice_in_dim(mesh_state, head_index * own_rows, own_rows, 0)
    hidden = own_state.astype(jnp.float32) + encoder_rows
    layer_qkv = qkv_rows(
        lax.all_gather(normalize(hidden).astype(jnp.bfloat16), "heads", axis=0, tiled=True),
        jnp.int32(0),
    )
    processor_queries = layer_qkv[:, :head_cols].reshape(mesh_len, local_heads, HS)
    processor_keys = layer_qkv[:, head_cols : 2 * head_cols].reshape(mesh_len, local_heads, HS)
    processor_values = layer_qkv[:, 2 * head_cols :].reshape(mesh_len, local_heads, HS)
    processor_scores = (
        jnp.einsum(
            "pws,iws->wpi", processor_queries, processor_keys, preferred_element_type=jnp.float32
        )
        * logit_scale_factor
    )
    layer_weights = jnp.exp(processor_scores)
    processor_probabilities = (
        layer_weights / jnp.sum(layer_weights, axis=-1, keepdims=True)
    ).astype(jnp.bfloat16)
    processor_context = jnp.einsum(
        "beq,qbo->ebo",
        processor_probabilities,
        processor_values,
        preferred_element_type=jnp.float32,
    ).astype(jnp.bfloat16)
    processor_context = processor_context.reshape(mesh_len, head_cols)
    layer_rows = lax.psum_scatter(
        jnp.dot(processor_context, w_out_proc, preferred_element_type=jnp.float32).astype(
            jnp.bfloat16
        ),
        "heads",
        scatter_dimension=0,
        tiled=True,
    ).astype(jnp.float32)
    return (hidden + layer_rows).astype(jnp.bfloat16)


def solution(mesh):
    return jax.shard_map(
        local,
        mesh=mesh,
        in_specs=(
            P(None, ("nodes", "heads")),
            P("nodes", None),
            P(),
            P(None, "heads"),
            P(None, "heads"),
            P(None, "heads"),
            P("heads", None),
            P(None, "heads"),
            P(None, "heads"),
            P(None, "heads"),
            P("heads", None),
            P("nodes", None, None),
            P("nodes", None),
            P("nodes", None),
        ),
        out_specs=P(("nodes", "heads"), None),
        check_vma=False,
    )
```

profile of v0, /device:TPU:1, one launch (start us, length us, event | category | flops | bytes accessed | tf_op | source)
XLA Modules:
  0.0 168.1 jit_solution(11767854757160667776)
XLA Ops:
  6.5 1.4 fusion.29
  8.0 0.3 multiply_reduce_fusion.2
  8.3 0.0 copy-start.11
  8.3 0.0 copy-start.10
  8.3 0.0 copy-start.2
  8.3 0.0 copy-start.4
  8.3 1.0 multiply_convert_fusion
  9.3 0.0 all-gather.2.cloned.1.call-update
  9.3 0.0 copy-start.9
  9.3 0.0 reduce-scatter.3.cloned.1.call-start
  9.4 0.1 convert_reduce_fusion
  9.6 0.2 fusion.7
  9.8 0.4 convolution_convert_fusion.8
  10.2 0.1 copy.32
  10.3 0.1 reshape.226
  10.4 0.1 copy.31
  10.6 23.0 %all-gather.2.cloned.1.call-done = bf16[512,1024]{1,0:T(8,128)(2,1)} async-done(((bf16[256,1024]{1,0:T(8,128)(2,1)}), bf16[512,1024]{1,0:T(8,128)(2,1)}) %all-gather.2.cloned.1.call-update) | async-done | bytes 1048592 | tf_op jit(solution)/shard_map/all_gather | solution.py:69
  33.6 2.1 %gather_fusion = bf16[32,1024]{1,0:T(8,128)(2,1)S(1)} fusion(bf16[512,1024]{1,0:T(8,128)(2,1)} %all-gather.2.cloned.1.call-done, s32[1024]{0:T(1024)S(1)} %pad_clamp_fusion.3), kind=kCustom, calls=%fused_computation | custom fusion | bytes 131200 | tf_op jit(solution)/shard_map/gather | solution.py:71
  35.7 2.1 %collective-permute-start = (bf16[32,1024]{1,0:T(8,128)(2,1)S(1)}, bf16[32,1024]{1,0:T(8,128)(2,1)S(1)}, u32[]{:S(2)}, u32[]{:S(2)}) collective-permute-start(bf16[32,1024]{1,0:T(8,128)(2,1)S(1)} %gather_fusion), channel_id=1, source_target_pairs={{510,0},{0,2},{2,4},{4,6},{6,8},{8,10},{10,12},{12,14},{14,16},{16... | collective-permute-start | bytes 196616 | tf_op jit(solution)/shard_map/ppermute | solution.py:16
  37.8 2.0 %gather_fusion.1 = bf16[32,1024]{1,0:T(8,128)(2,1)S(1)} fusion(bf16[512,1024]{1,0:T(8,128)(2,1)} %all-gather.2.cloned.1.call-done, s32[1024]{0:T(1024)S(1)} %pad_clamp_fusion.2), kind=kCustom, calls=%fused_computation.1 | custom fusion | bytes 131200 | tf_op jit(solution)/shard_map/gather | solution.py:71
  39.9 8.8 %collective-permute-start.1 = (bf16[32,1024]{1,0:T(8,128)(2,1)S(1)}, bf16[32,1024]{1,0:T(8,128)(2,1)S(1)}, u32[]{:S(2)}, u32[]{:S(2)}) collective-permute-start(bf16[32,1024]{1,0:T(8,128)(2,1)S(1)} %gather_fusion.1), channel_id=1, source_target_pairs={{2,0},{4,2},{6,4},{8,6},{10,8},{12,10},{14,12},{16,14},{18,16},{20... | collective-permute-start | bytes 196616 | tf_op jit(solution)/shard_map/ppermute | solution.py:16
  48.7 0.6 gather_fusion.2
  49.3 1.9 %collective-permute-start.2 = (bf16[32,1024]{1,0:T(8,128)(2,1)S(1)}, bf16[32,1024]{1,0:T(8,128)(2,1)S(1)}, u32[]{:S(2)}, u32[]{:S(2)}) collective-permute-start(bf16[32,1024]{1,0:T(8,128)(2,1)S(1)} %gather_fusion.2), channel_id=1, source_target_pairs={{508,0},{510,2},{0,4},{2,6},{4,8},{6,10},{8,12},{10,14},{12,16},{1... | collective-permute-start | bytes 196616 | tf_op jit(solution)/shard_map/ppermute | solution.py:16
  51.3 0.6 gather_fusion.3
  51.9 9.1 %collective-permute-start.3 = (bf16[32,1024]{1,0:T(8,128)(2,1)S(1)}, bf16[32,1024]{1,0:T(8,128)(2,1)S(1)}, u32[]{:S(2)}, u32[]{:S(2)}) collective-permute-start(bf16[32,1024]{1,0:T(8,128)(2,1)S(1)} %gather_fusion.3), channel_id=1, source_target_pairs={{4,0},{6,2},{8,4},{10,6},{12,8},{14,10},{16,12},{18,14},{20,16},{2... | collective-permute-start | bytes 196616 | tf_op jit(solution)/shard_map/ppermute | solution.py:16
  61.0 0.1 constant_dynamic-update-slice_fusion.4
  61.1 1.2 collective-permute-done.3
  62.3 1.1 convolution_convert_fusion
  63.4 0.2 copy-done.12
  63.5 1.1 convolution_convert_fusion.1
  64.6 1.2 pad_maximum_fusion
  65.8 1.6 copy.33
  67.4 18.3 %gather_fusion.4 = bf16[4096,1024]{1,0:T(8,128)(2,1)} fusion(bf16[640,1024]{1,0:T(8,128)(2,1)S(1)} %copy.33, s32[4096]{0:T(1024)S(1)} %broadcast_clamp_fusion), kind=kCustom, calls=%fused_computation.4 | custom fusion | bytes 16793600 | tf_op jit(solution)/shard_map/gather | solution.py:78
  85.6 6.0 %fusion.28 = (bf16[128,32,512]{2,1,0:T(8,128)(2,1)}, bf16[128,32,512]{2,1,0:T(8,128)(2,1)}) fusion(bf16[128,32,1024]{2,1,0:T(8,128)(2,1)} %bitcast.54), kind=kLoop, calls=%fused_computation.77 | loop fusion | bytes 16777216 | tf_op jit(solution)/shard_map/slice | solution.py:79
  91.7 7.9 %copy.54 = bf16[128,32,512]{0,2,1:T(8,128)(2,1)} copy(bf16[128,32,512]{2,1,0:T(8,128)(2,1)} %get-tuple-element.5) | data formatting | bytes 8388608
  99.5 3.8 %multiply_reduce_fusion.1 = f32[128,8,32]{0,1,2:T(8,128)S(1)} fusion(f32[128,8,64]{0,2,1:T(8,128)S(1)} %bitcast_convert_fusion, bf16[128,32,512]{0,2,1:T(8,128)(2,1)} %copy.54), kind=kLoop, calls=%fused_computation.7 | loop fusion | flops 6258688 | bytes 4587520
  103.3 0.1 fusion.4
  103.4 0.1 copy.57
  103.5 7.9 %copy.55 = bf16[128,32,512]{0,2,1:T(8,128)(2,1)} copy(bf16[128,32,512]{2,1,0:T(8,128)(2,1)} %get-tuple-element.6) | data formatting | bytes 8388608
  111.4 3.3 %multiply_reduce_fusion = bf16[128,8,64]{0,2,1:T(8,128)(2,1)S(1)} fusion(bf16[128,8,32,64]{0,3,1,2:T(8,128)(2,1)} %bitcast.55, f32[128,8,32]{0,1,2:T(8,128)S(1)} %copy.57), kind=kLoop, calls=%fused_computation.6 | loop fusion | flops 6225920 | bytes 4456448 | tf_op jit(solution)/shard_map/nhf,nfhd->nhd/dot_general | solution.py:87
  114.7 0.0 copy-start.6
  114.7 1.0 convolution_convert_fusion.3
  115.7 0.0 reduce-scatter.3.cloned.1.call-update
  115.8 0.0 reduce-scatter.5.cloned.1.call-start
  115.8 16.8 %reduce-scatter.3.cloned.1.call-done = bf16[64,1024]{1,0:T(8,128)(2,1)} async-done(((bf16[128,1024]{1,0:T(8,128)(2,1)}), bf16[64,1024]{1,0:T(8,128)(2,1)}) %reduce-scatter.3.cloned.1.call-update) | async-done | bytes 131088 | tf_op jit(solution)/shard_map/reduce_scatter | solution.py:105
  132.6 1.0 fusion.13
  133.7 1.1 multiply_reduce_fusion.3
  134.8 1.0 multiply_convert_fusion.1
  135.8 2.0 %all_gather.7 = bf16[128,1024]{1,0:T(8,128)(2,1)S(1)} all-gather(bf16[64,1024]{1,0:T(8,128)(2,1)S(1)} %multiply_convert_fusion.1), channel_id=1, replica_groups=mesh['nodes'=256,'heads'=2] {'heads'}, dimensions={0}, use_global_device_ids=true | all-gather | bytes 393216 | tf_op jit(solution)/shard_map/all_gather | solution.py:114
  137.8 0.3 convolution_convert_fusion.6
  138.1 0.0 copy-start.7
  138.1 0.1 copy.37
  138.2 1.6 convolution_convert_fusion.5
  139.9 0.1 copy.38
  140.0 0.3 convolution_convert_fusion.7
  140.3 0.1 copy.36
  140.4 0.0 copy-start.8
  140.4 0.3 fusion.1
  140.7 0.2 convolution_convert_fusion.4
  141.0 0.7 copy-done.8
  141.7 1.0 convolution_convert_fusion.2
  142.7 0.0 reduce-scatter.5.cloned.1.call-update
  142.7 17.3 %reduce-scatter.5.cloned.1.call-done = bf16[64,1024]{1,0:T(8,128)(2,1)} async-done(((bf16[128,1024]{1,0:T(8,128)(2,1)}), bf16[64,1024]{1,0:T(8,128)(2,1)}) %reduce-scatter.5.cloned.1.call-update) | async-done | bytes 131088 | tf_op jit(solution)/shard_map/reduce_scatter | solution.py:137
  160.0 1.6 add_convert_fusion
  (39 shorter events, 0.2 us)
Async XLA Ops:
  6.5 55.8 %copy-start = (bf16[1024,512]{1,0:T(8,128)(2,1)S(1)}, bf16[1024,512]{1,0:T(8,128)(2,1)}, u32[]{:S(2)}) copy-start(bf16[1024,512]{1,0:T(8,128)(2,1)} %param.19) | copy-start | bytes 3145732
  6.5 27.1 %all-gather.2.cloned.1.call-start = ((), (), s32[]{:S(2)}) async-start(), calls=%async_computation.2 | async-start | bytes 1572864 | tf_op jit(solution)/shard_map/all_gather | solution.py:69
  8.3 1.1 copy-start.11
  8.3 1.2 copy-start.10
  8.3 1.2 copy-start.2
  8.3 1.5 copy-start.4
  9.3 1.2 copy-start.9
  9.3 123.3 %reduce-scatter.3.cloned.1.call-start = ((), (), s32[]{:S(2)}) async-start(), calls=%async_computation.3 | async-start | bytes 393216 | tf_op jit(solution)/shard_map/reduce_scatter | solution.py:105
  33.6 15.1 %copy-start.1 = (bf16[512,1024]{1,0:T(8,128)(2,1)S(1)}, bf16[512,1024]{1,0:T(8,128)(2,1)}, u32[]{:S(2)}) copy-start(bf16[512,1024]{1,0:T(8,128)(2,1)} %all-gather.2.cloned.1.call-done) | copy-start | bytes 3145732
  35.7 25.3 %collective-permute-start = (bf16[32,1024]{1,0:T(8,128)(2,1)S(1)}, bf16[32,1024]{1,0:T(8,128)(2,1)S(1)}, u32[]{:S(2)}, u32[]{:S(2)}) collective-permute-start(bf16[32,1024]{1,0:T(8,128)(2,1)S(1)} %gather_fusion), channel_id=1, source_target_pairs={{510,0},{0,2},{2,4},{4,6},{6,8},{8,10},{10,12},{12,14},{14,16},{16... | collective-permute-start | bytes 196616 | tf_op jit(solution)/shard_map/ppermute | solution.py:16
  39.9 21.2 %collective-permute-start.1 = (bf16[32,1024]{1,0:T(8,128)(2,1)S(1)}, bf16[32,1024]{1,0:T(8,128)(2,1)S(1)}, u32[]{:S(2)}, u32[]{:S(2)}) collective-permute-start(bf16[32,1024]{1,0:T(8,128)(2,1)S(1)} %gather_fusion.1), channel_id=1, source_target_pairs={{2,0},{4,2},{6,4},{8,6},{10,8},{12,10},{14,12},{16,14},{18,16},{20... | collective-permute-start | bytes 196616 | tf_op jit(solution)/shard_map/ppermute | solution.py:16
  49.3 11.8 %collective-permute-start.2 = (bf16[32,1024]{1,0:T(8,128)(2,1)S(1)}, bf16[32,1024]{1,0:T(8,128)(2,1)S(1)}, u32[]{:S(2)}, u32[]{:S(2)}) collective-permute-start(bf16[32,1024]{1,0:T(8,128)(2,1)S(1)} %gather_fusion.2), channel_id=1, source_target_pairs={{508,0},{510,2},{0,4},{2,6},{4,8},{6,10},{8,12},{10,14},{12,16},{1... | collective-permute-start | bytes 196616 | tf_op jit(solution)/shard_map/ppermute | solution.py:16
  51.9 10.4 %collective-permute-start.3 = (bf16[32,1024]{1,0:T(8,128)(2,1)S(1)}, bf16[32,1024]{1,0:T(8,128)(2,1)S(1)}, u32[]{:S(2)}, u32[]{:S(2)}) collective-permute-start(bf16[32,1024]{1,0:T(8,128)(2,1)S(1)} %gather_fusion.3), channel_id=1, source_target_pairs={{4,0},{6,2},{8,4},{10,6},{12,8},{14,10},{16,12},{18,14},{20,16},{2... | collective-permute-start | bytes 196616 | tf_op jit(solution)/shard_map/ppermute | solution.py:16
  62.3 1.2 copy-start.12
  111.4 3.3 %copy-start.5 = (bf16[512,1024]{1,0:T(8,128)(2,1)S(1)}, bf16[512,1024]{1,0:T(8,128)(2,1)}, u32[]{:S(2)}) copy-start(bf16[512,1024]{1,0:T(8,128)(2,1)} %param.20) | copy-start | bytes 3145732
  114.7 23.1 %copy-start.6 = (bf16[1024,512]{1,0:T(8,128)(2,1)S(1)}, bf16[1024,512]{1,0:T(8,128)(2,1)}, u32[]{:S(2)}) copy-start(bf16[1024,512]{1,0:T(8,128)(2,1)} %param.21) | copy-start | bytes 3145732
  115.8 44.2 %reduce-scatter.5.cloned.1.call-start = ((), (), s32[]{:S(2)}) async-start(), calls=%async_computation.4 | async-start | bytes 393216 | tf_op jit(solution)/shard_map/reduce_scatter | solution.py:137
  138.1 1.9 %copy-start.7 = (bf16[1024,512]{1,0:T(8,128)(2,1)S(1)}, bf16[1024,512]{1,0:T(8,128)(2,1)}, u32[]{:S(2)}) copy-start(bf16[1024,512]{1,0:T(8,128)(2,1)} %param.23) | copy-start | bytes 3145732
  140.4 1.2 copy-start.8
  141.0 19.0 %copy-start.3 = (bf16[64,1024]{1,0:T(8,128)(2,1)S(1)}, bf16[64,1024]{1,0:T(8,128)(2,1)}, u32[]{:S(2)}) copy-start(bf16[64,1024]{1,0:T(8,128)(2,1)} %reduce-scatter.3.cloned.1.call-done) | copy-start | bytes 393220
Sparse Core Ops, SparseCore 0:
  9.4 24.0 all-gather.1
  115.9 16.6 reduce-scatter.2
  142.8 17.0 reduce-scatter.4
where the time goes:
time: 169 us; the launch traced here: 168 us
  waiting for transfers between devices  58.3 us (34%)
  local copies, waits for them, and re-layouts  48.8 us (29%)
  starting transfers between devices  22 us (13%)
  other arithmetic  14.8 us (9%)
  between operations  13.6 us (8%)
  matrix products  8.7 us (5%)
  blocking collectives  1.99 us (1%)
    all_gather x1, waiting for transfers between devices, local(): region = lax.all_gather(embedded, 'heads', axis=0, tiled=True)  23 us
    ppermute x4, starting transfers between devices, passed_along(): return lax.ppermute(block, axis, route)  21.9 us
    gather x1, local copies, waits for them, and re-layouts, local(): picked = kv_table[edge_senders]  18.3 us
    reduce_scatter x1, waiting for transfers between devices, local(): lax.psum_scatter(jnp.dot(processor_context, w_out_proc, preferred_element...  17.3 us
    unnamed x33, local copies, waits for them, and re-layouts  16.8 us
    reduce_scatter x1, waiting for transfers between devices, local(): lax.psum_scatter(jnp.dot(enc_context, w_out_enc, preferred_element_type=j...  16.8 us
    slice x1, local copies, waits for them, and re-layouts, local(): picked[:, :, :head_cols].reshape(mesh_len, fan_slots, local_heads, HS)  6.04 us
    gather x4, local copies, waits for them, and re-layouts, local(): outgoing = region[listed_rows[slot]]  5.42 us
  transfers between devices with their start and end apart: 7, of which 4 were waited for; matrix products, arithmetic and copies ran while one was open for 3% of the time, Pallas kernels for 0%

commit v1 on v0

v1 whole, which is shorter than its diff:
```python
import functools
import math

import jax
import jax.numpy as jnp
from jax import lax
from jax.experimental import pallas as pl
from jax.experimental.pallas import tpu as pltpu
from jax.sharding import PartitionSpec as P

HEADS = 16
HS = 64
NEIGH = 4
F32 = jnp.float32
BF16 = jnp.bfloat16
MESH = pl.DeviceIdType.MESH
LANES = 128
LOG2E = math.log2(math.e)
NN = (((1,), (0,)), ((), ()))
NT = (((1,), (1,)), ((), ()))


def offset_of(slot):
    return (slot // 2 + 1) * (1 if slot % 2 == 0 else -1)


def dot(a, b, dims=NN):
    return lax.dot_general(a, b, dims, preferred_element_type=F32)


def split(x):
    high = x.astype(BF16)
    return high, (x - high.astype(F32)).astype(BF16)


def normalize(x):
    centred = x - jnp.mean(x, axis=-1, keepdims=True)
    spread = jnp.mean(centred * centred, axis=-1, keepdims=True)
    return centred * lax.rsqrt(spread + 1e-05)


def iota(shape, axis):
    return lax.broadcasted_iota(jnp.int32, shape, axis)


def kernel(
    fields, mesh_state, w_embed, w_q, w_k, w_v, w_o, p_q, p_k, p_v, p_o, send_rows, senders, mask,
    out,
    own_v, mesh_v, embed_v, wq_v, wk_v, wv_v, wo_v, pq_v, pk_v, pv_v, po_v, rows_v, send_v, mask_v,
    other_v, listed, received, table, bias, weights_k, weights_v, queries, hidden, sums_out, sums_in,
    context, last_out, last_in,
    load_sem, half_sem, list_send, list_recv, sum_send, sum_recv, last_sem,
):
    n = lax.axis_size("nodes")
    region, core = lax.axis_index("nodes"), lax.axis_index("heads")
    twin = {"nodes": region, "heads": 1 - core}
    ch, half = fields.shape
    nodes, width = mesh_state.shape
    fan = senders.shape[1]
    cols = w_q.shape[1]
    pairs = cols // LANES
    cap = send_rows.shape[2]
    points = 2 * half
    remote = NEIGH * cap
    own_rows = nodes // 2
    chunk = width // 4

    def neighbour(slot, other):
        place = lax.rem(region + (offset_of(slot) + n), n)
        return {"nodes": place, "heads": 1 - core if other else core}

    barrier = pltpu.get_barrier_semaphore()
    pl.semaphore_signal(barrier, inc=1, device_id=twin, device_id_type=MESH)
    for slot in range(NEIGH):
        for other in range(2):
            pl.semaphore_signal(
                barrier, inc=1, device_id=neighbour(slot, other), device_id_type=MESH
            )

    loads = {}
    pieces = [
        (fields, own_v), (send_rows, rows_v), (w_embed, embed_v), (w_k, wk_v), (w_v, wv_v),
        (senders, send_v), (mask, mask_v), (mesh_state, mesh_v), (w_q, wq_v), (w_o, wo_v),
        (p_q, pq_v), (p_k, pk_v), (p_v, pv_v), (p_o, po_v),
    ]
    for index, (source, target) in enumerate(pieces):
        loads[id(target)] = pltpu.make_async_copy(source, target, load_sem.at[index])
        loads[id(target)].start()

    def loaded(*targets):
        for target in targets:
            loads[id(target)].wait()

    loaded(own_v, rows_v)
    widen = (iota((LANES, ch), 0) == iota((LANES, ch), 1)).astype(BF16)
    own = dot(widen, own_v[...]).astype(BF16)
    table[0:LANES, 0:half] = own
    table[LANES : 2 * LANES, 0:half] = own
    rows = rows_v[0]
    wanted = jnp.concatenate([rows[j : j + 1, :] for j in range(NEIGH)], axis=1) - core * half
    pick = (iota((half, remote), 0) == wanted).astype(BF16)
    listed[...] = dot(own, pick).T.astype(BF16)
    pl.semaphore_wait(barrier, 1 + 2 * NEIGH)
    half_copy = pltpu.make_async_remote_copy(
        src_ref=fields, dst_ref=other_v, send_sem=half_sem.at[0], recv_sem=half_sem.at[1],
        device_id=twin, device_id_type=MESH,
    )
    half_copy.start()
    list_copies = []
    for slot in range(NEIGH):
        for other in range(2):
            part = pl.ds(slot * cap, cap)
            list_copies.append(
                pltpu.make_async_remote_copy(
                    src_ref=listed.at[part], dst_ref=received.at[other, part],
                    send_sem=list_send.at[2 * slot + other],
                    recv_sem=list_recv.at[2 * slot + other],
                    device_id=neighbour(slot, other), device_id_type=MESH,
                )
            )
            list_copies[-1].start()

    loaded(embed_v)
    embed = dot(widen, embed_v[...])
    embed = embed - jnp.mean(embed, axis=-1, keepdims=True)
    embed = jnp.concatenate(split(embed), axis=0)
    gram = dot(embed, embed, NT) * (1.0 / width)
    gram = gram[:LANES] + gram[LANES:]
    gram = jnp.concatenate(split(gram[:, :LANES] + gram[:, LANES:]), axis=1)
    loaded(wk_v, wv_v)
    for weight, target in ((wk_v, weights_k), (wv_v, weights_v)):
        both = dot(embed, weight[...])
        high, low = split(both[:LANES] + both[LANES:])
        target[0] = high
        target[1] = low

    loaded(send_v, mask_v)
    block = 32
    place = iota((1, points), 1)
    place = jnp.where(place < half, place + core * half, place - core * half)
    place = jnp.concatenate([place, iota((1, remote), 1) + points], axis=1)

    def count(step, carry):
        part = pl.ds(pl.multiple_of(step * block, block), block)
        live = jnp.where(mask_v[part, :] > 0, send_v[part, :], -1)
        total = jnp.zeros((block, points + remote), F32)
        for slot in range(fan):
            total += (live[:, slot : slot + 1] == place).astype(F32)
        bias[part, :] = jnp.where(total > 0, jnp.log2(jnp.maximum(total, 1.0)), -1e30)
        return carry

    lax.fori_loop(0, nodes // block, count, 0)

    loaded(mesh_v, wq_v)
    normed = normalize(mesh_v[...].astype(F32)).astype(BF16)
    enc_queries = dot(normed, wq_v[...]).astype(BF16)
    low_lanes = iota((nodes, LANES), 1) < HS
    for pair in range(pairs):
        lanes = slice(pair * LANES, (pair + 1) * LANES)
        two = enc_queries[:, lanes]
        even = jnp.where(low_lanes, two, jnp.zeros_like(two))
        odd = jnp.where(low_lanes, jnp.zeros_like(two), two)
        two = jnp.concatenate([even, odd], axis=0)
        spread = dot(two, weights_k[0, :, lanes], NT) + dot(two, weights_k[1, :, lanes], NT)
        high, low = split(spread)
        queries[pair, :, 0:LANES] = high
        queries[pair, :, LANES : 2 * LANES] = low

    half_copy.wait()
    other = dot(widen, other_v[...]).astype(BF16)
    table[0:LANES, half:points] = other
    table[LANES : 2 * LANES, half:points] = other
    for copy in list_copies:
        copy.wait()
    far = (received[0].astype(F32) + received[1].astype(F32)).T.astype(BF16)
    table[0:LANES, points : points + remote] = far
    table[LANES : 2 * LANES, points : points + remote] = far
    squares = dot(gram, table[...]) * table[0:LANES, :].astype(F32)
    squares = jnp.maximum(jnp.sum(squares, axis=0, keepdims=True), 0.0)
    inverse = lax.rsqrt(squares + 1e-05)
    logit_scale = inverse * (LOG2E / math.sqrt(HS))

    loaded(wo_v)
    points_last = table[0:LANES, :]
    edges = bias[...]
    edges = jnp.concatenate([edges, edges], axis=0)
    for pair in range(pairs):
        lanes = slice(pair * LANES, (pair + 1) * LANES)
        logits = dot(queries[pair], table[...]) * logit_scale + edges
        logits = jnp.exp2(logits - jnp.max(logits, axis=-1, keepdims=True))
        total = jnp.sum(logits, axis=-1, keepdims=True)
        mixed = dot((logits * inverse).astype(BF16), points_last, NT) / total
        high, low = split(mixed)
        both = (
            dot(high, weights_v[0, :, lanes])
            + dot(high, weights_v[1, :, lanes])
            + dot(low, weights_v[0, :, lanes])
        )
        context[:, lanes] = jnp.where(low_lanes, both[:nodes], both[nodes:]).astype(BF16)

    sum_copies = []
    for step in range(4):
        lanes = slice(step * chunk, (step + 1) * chunk)
        part = dot(context[...], wo_v[:, lanes])
        sums_out[step] = part.astype(BF16)
        sum_copies.append(
            pltpu.make_async_remote_copy(
                src_ref=sums_out.at[step], dst_ref=sums_in.at[step],
                send_sem=sum_send.at[step], recv_sem=sum_recv.at[step],
                device_id=twin, device_id_type=MESH,
            )
        )
        sum_copies[-1].start()
        hidden[:, lanes] = mesh_v[:, lanes].astype(F32) + part
    for step in range(4):
        lanes = slice(step * chunk, (step + 1) * chunk)
        sum_copies[step].wait()
        hidden[:, lanes] += sums_in[step].astype(F32)

    normed = normalize(hidden[...]).astype(BF16)
    loaded(pq_v, pk_v, pv_v)
    proc_q = dot(normed, pq_v[...]).astype(BF16)
    proc_k = dot(normed, pk_v[...]).astype(BF16)
    proc_v = dot(normed, pv_v[...]).astype(BF16)
    for pair in range(pairs):
        lanes = slice(pair * LANES, (pair + 1) * LANES)
        two = proc_q[:, lanes]
        even = jnp.where(low_lanes, two, jnp.zeros_like(two))
        odd = jnp.where(low_lanes, jnp.zeros_like(two), two)
        two = jnp.concatenate([even, odd], axis=0)
        logits = dot(two, proc_k[:, lanes], NT) * (LOG2E / math.sqrt(HS))
        logits = jnp.exp2(logits - jnp.max(logits, axis=-1, keepdims=True))
        probs = (logits / jnp.sum(logits, axis=-1, keepdims=True)).astype(BF16)
        both = dot(probs, proc_v[:, lanes])
        context[:, lanes] = jnp.where(low_lanes, both[:nodes], both[nodes:]).astype(BF16)

    loaded(po_v)
    theirs = pl.ds(pl.multiple_of((1 - core) * own_rows, own_rows), own_rows)
    mine = pl.ds(pl.multiple_of(core * own_rows, own_rows), own_rows)
    last_out[...] = dot(context[theirs, :], po_v[...]).astype(BF16)
    last = pltpu.make_async_remote_copy(
        src_ref=last_out, dst_ref=last_in, send_sem=last_sem.at[0], recv_sem=last_sem.at[1],
        device_id=twin, device_id_type=MESH,
    )
    last.start()
    part = hidden[mine, :] + dot(context[mine, :], po_v[...])
    last.wait()
    out[...] = (part + last_in[...].astype(F32)).astype(BF16)


def local(*args):
    fields, mesh_state = args[0], args[1]
    send_rows, senders = args[11], args[12]
    ch, half = fields.shape
    nodes, width = mesh_state.shape
    cols = args[3].shape[1]
    pairs = cols // LANES
    remote = send_rows.shape[1] * send_rows.shape[2]
    columns = 2 * half + remote
    copies = [pltpu.VMEM(x.shape, x.dtype) for x in args]
    buffers = [
        pltpu.VMEM((ch, half), BF16),
        pltpu.VMEM((remote, LANES), BF16),
        pltpu.VMEM((2, remote, LANES), BF16),
        pltpu.VMEM((2 * LANES, columns), BF16),
        pltpu.VMEM((nodes, columns), F32),
        pltpu.VMEM((2, LANES, cols), BF16),
        pltpu.VMEM((2, LANES, cols), BF16),
        pltpu.VMEM((pairs, 2 * nodes, 2 * LANES), BF16),
        pltpu.VMEM((nodes, width), F32),
        pltpu.VMEM((4, nodes, width // 4), BF16),
        pltpu.VMEM((4, nodes, width // 4), BF16),
        pltpu.VMEM((nodes, cols), BF16),
        pltpu.VMEM((nodes // 2, width), BF16),
        pltpu.VMEM((nodes // 2, width), BF16),
    ]
    semaphores = [
        pltpu.SemaphoreType.DMA((len(args),)),
        pltpu.SemaphoreType.DMA((2,)),
        pltpu.SemaphoreType.DMA((2 * NEIGH,)),
        pltpu.SemaphoreType.DMA((2 * NEIGH,)),
        pltpu.SemaphoreType.DMA((4,)),
        pltpu.SemaphoreType.DMA((4,)),
        pltpu.SemaphoreType.DMA((2,)),
    ]
    return pl.pallas_call(
        kernel,
        out_shape=jax.ShapeDtypeStruct((nodes // 2, width), BF16),
        in_specs=[pl.BlockSpec(memory_space=pl.ANY)] * len(args),
        out_specs=pl.BlockSpec(memory_space=pltpu.VMEM),
        scratch_shapes=copies + buffers + semaphores,
        compiler_params=pltpu.CompilerParams(
            collective_id=0, has_side_effects=True, vmem_limit_bytes=48 * 1024 * 1024
        ),
        cost_estimate=pl.CostEstimate(
            flops=3_000_000_000, bytes_accessed=9_500_000, transcendentals=800_000
        ),
        name="encode_and_process",
    )(*args)


def solution(mesh):
    return jax.shard_map(
        local,
        mesh=mesh,
        in_specs=(
            P(None, ("nodes", "heads")),
            P("nodes", None),
            P(),
            P(None, "heads"),
            P(None, "heads"),
            P(None, "heads"),
            P("heads", None),
            P(None, "heads"),
            P(None, "heads"),
            P(None, "heads"),
            P("heads", None),
            P("nodes", None, None),
            P("nodes", None),
            P("nodes", None),
        ),
        out_specs=P(("nodes", "heads"), None),
        check_vma=False,
    )
```

time: 169 us -> 38.9 us (0.23)
  waiting for transfers between devices: 58.3 us -> 0 us
  local copies, waits for them, and re-layouts: 48.8 us -> 10.3 us
  Pallas kernels: 0 us -> 28.1 us
  starting transfers between devices: 22 us -> 0 us
  other arithmetic: 14.8 us -> 0 us
  between operations: 13.6 us -> 0.04 us
  matrix products: 8.7 us -> 0 us
  blocking collectives: 1.99 us -> 0 us
    reduce_scatter x2 -> x0, waiting for transfers between devices: 34.1 us -> none  [the longest x1 17.3 us: local(): lax.psum_scatter(jnp.dot(processor_context, w_out_proc, preferred_element...]
    pallas_call x0 -> x1, Pallas kernels: none -> 28.1 us  [local(): pl.pallas_call(kernel, out_shape=jax.ShapeDtypeStruct((nodes // 2, width)...]
    gather x5 -> x0, local copies, waits for them, and re-layouts: 23.7 us -> none  [the longest x1 18.3 us: local(): picked = kv_table[edge_senders]]
    all_gather x1 -> x0, waiting for transfers between devices: 23 us -> none  [local(): region = lax.all_gather(embedded, 'heads', axis=0, tiled=True)]
    ppermute x4 -> x0, starting transfers between devices: 21.9 us -> none  [passed_along(): return lax.ppermute(block, axis, route)]
    dot_general x11 -> x0, matrix products: 8.7 us -> none  [the longest x1 1.6 us: qkv_rows(): jnp.dot(shard_rows, w_key_proc, preferred_element_type=jnp.float32)]
    unnamed x33 -> x23, local copies, waits for them, and re-layouts: 16.8 us -> 10.3 us
    slice x1 -> x0, local copies, waits for them, and re-layouts: 6.04 us -> none  [local(): picked[:, :, :head_cols].reshape(mesh_len, fan_slots, local_heads, HS)]
  transfers between devices with their start and end apart: 7 -> 0, of which waited for: 4 -> 0; matrix products, arithmetic and copies ran while one was open for 3% -> 0% of each run, Pallas kernels for 0% -> 0%
where the time goes in v1:
time: 38.9 us; the launch traced here: 38.4 us
  Pallas kernels  28.1 us (72%)
  local copies, waits for them, and re-layouts  10.3 us (26%)
    pallas_call x1, Pallas kernels, local(): pl.pallas_call(kernel, out_shape=jax.ShapeDtypeStruct((nodes // 2, width)...  28.1 us
    unnamed x23, local copies, waits for them, and re-layouts  10.3 us

profile of v1, /device:TPU:1, one launch (start us, length us, event | category | flops | bytes accessed | tf_op | source)
XLA Modules:
  0.0 38.4 jit_solution(5671643243306302270)
XLA Ops:
  0.0 0.0 copy-start.9
  0.0 0.8 %copy.15.senders = s32[128,32]{1,0:T(8,128)S(1)} copy(s32[128,32]{0,1:T(8,128)} %param.26) | data formatting | bytes 32768 | tf_op args[12]
  0.8 0.0 copy-done.9
  0.8 0.0 copy-start.7
  0.8 0.0 copy-start.8
  0.9 0.1 copy.16.mask
  1.0 0.7 %copy-done.7 = bf16[100,256]{1,0:T(8,128)(2,1)S(1)} copy-done((bf16[100,256]{1,0:T(8,128)(2,1)S(1)}, bf16[100,256]{1,0:T(8,128)(2,1)}, u32[]{:S(2)}) %copy-start.7) | copy-done | bytes 51224
  1.7 0.0 copy-done.8
  1.7 0.0 copy-start
  1.7 1.2 %copy-done = bf16[1024,512]{1,0:T(8,128)(2,1)S(1)} copy-done((bf16[1024,512]{1,0:T(8,128)(2,1)S(1)}, bf16[1024,512]{1,0:T(8,128)(2,1)}, u32[]{:S(2)}) %copy-start) | copy-done | bytes 1048600
  2.9 0.0 copy-start.1
  2.9 1.2 %copy-done.1 = bf16[1024,512]{1,0:T(8,128)(2,1)S(1)} copy-done((bf16[1024,512]{1,0:T(8,128)(2,1)S(1)}, bf16[1024,512]{1,0:T(8,128)(2,1)}, u32[]{:S(2)}) %copy-start.1) | copy-done | bytes 1048600
  4.1 0.0 copy-start.2
  4.1 1.2 %copy-done.2 = bf16[1024,512]{1,0:T(8,128)(2,1)S(1)} copy-done((bf16[1024,512]{1,0:T(8,128)(2,1)S(1)}, bf16[1024,512]{1,0:T(8,128)(2,1)}, u32[]{:S(2)}) %copy-start.2) | copy-done | bytes 1048600
  5.3 0.0 copy-start.3
  5.3 1.2 %copy-done.3 = bf16[512,1024]{1,0:T(8,128)(2,1)S(1)} copy-done((bf16[512,1024]{1,0:T(8,128)(2,1)S(1)}, bf16[512,1024]{1,0:T(8,128)(2,1)}, u32[]{:S(2)}) %copy-start.3) | copy-done | bytes 1048600
  6.6 0.0 copy-start.4
  6.6 1.2 %copy-done.4 = bf16[1024,512]{1,0:T(8,128)(2,1)S(1)} copy-done((bf16[1024,512]{1,0:T(8,128)(2,1)S(1)}, bf16[1024,512]{1,0:T(8,128)(2,1)}, u32[]{:S(2)}) %copy-start.4) | copy-done | bytes 1048600
  7.8 0.0 copy-start.5
  7.8 0.9 %copy-done.5 = bf16[128,1024]{1,0:T(8,128)(2,1)S(1)} copy-done((bf16[128,1024]{1,0:T(8,128)(2,1)S(1)}, bf16[128,1024]{1,0:T(8,128)(2,1)}, u32[]{:S(2)}) %copy-start.5) | copy-done | bytes 262168
  8.7 0.0 copy-start.6
  8.7 0.9 %copy-done.6 = bf16[100,1024]{1,0:T(8,128)(2,1)S(1)} copy-done((bf16[100,1024]{1,0:T(8,128)(2,1)S(1)}, bf16[100,1024]{1,0:T(8,128)(2,1)}, u32[]{:S(2)}) %copy-start.6) | copy-done | bytes 204824
  9.7 28.1 %encode_and_process.1 = bf16[64,1024]{1,0:T(8,128)(2,1)S(1)} custom-call(bf16[100,256]{1,0:T(8,128)(2,1)S(1)} %copy-done.7, bf16[128,1024]{1,0:T(8,128)(2,1)S(1)} %copy-done.5, bf16[100,1024]{1,0:T(8,128)(2,1)S(1)} %copy-done.6, bf16[1024,512]{1,0:T(8,128)(2,1)S(1)} %copy-done, bf16[1024,512]{1,0:T(8,128)(2,1)S(1)} %copy-done.1, ...), custom_call_target="tpu_custom_call" | custom-call | flops 3000000000 | bytes 9500000 | tf_op jit(solution)/shard_map/encode_and_process/pallas_call | solution.py:286
  37.7 0.7 %copy.18 = bf16[64,1024]{1,0:T(8,128)(2,1)} copy(bf16[64,1024]{1,0:T(8,128)(2,1)S(1)} %encode_and_process.1) | data formatting | bytes 262144
Async XLA Ops:
  0.0 0.8 %copy-start.9 = (s32[128,32]{0,1:T(8,128)S(1)}, s32[128,32]{0,1:T(8,128)}, u32[]{:S(2)}) copy-start(s32[128,32]{0,1:T(8,128)} %param.27) | copy-start | bytes 49156
  0.8 0.8 %copy-start.7 = (bf16[100,256]{1,0:T(8,128)(2,1)S(1)}, bf16[100,256]{1,0:T(8,128)(2,1)}, u32[]{:S(2)}) copy-start(bf16[100,256]{1,0:T(8,128)(2,1)} %fields.1) | copy-start | bytes 153604
  0.8 0.8 %copy-start.8 = (s32[1,4,32]{2,1,0:T(4,128)S(1)}, s32[1,4,32]{2,1,0:T(4,128)}, u32[]{:S(2)}) copy-start(s32[1,4,32]{2,1,0:T(4,128)} %send_rows.1) | copy-start | bytes 1540
  1.7 1.2 %copy-start = (bf16[1024,512]{1,0:T(8,128)(2,1)S(1)}, bf16[1024,512]{1,0:T(8,128)(2,1)}, u32[]{:S(2)}) copy-start(bf16[1024,512]{1,0:T(8,128)(2,1)} %w_q.1) | copy-start | bytes 3145732
  2.9 1.2 %copy-start.1 = (bf16[1024,512]{1,0:T(8,128)(2,1)S(1)}, bf16[1024,512]{1,0:T(8,128)(2,1)}, u32[]{:S(2)}) copy-start(bf16[1024,512]{1,0:T(8,128)(2,1)} %w_k.1) | copy-start | bytes 3145732
  4.1 1.2 %copy-start.2 = (bf16[1024,512]{1,0:T(8,128)(2,1)S(1)}, bf16[1024,512]{1,0:T(8,128)(2,1)}, u32[]{:S(2)}) copy-start(bf16[1024,512]{1,0:T(8,128)(2,1)} %w_v.1) | copy-start | bytes 3145732
  5.3 1.2 %copy-start.3 = (bf16[512,1024]{1,0:T(8,128)(2,1)S(1)}, bf16[512,1024]{1,0:T(8,128)(2,1)}, u32[]{:S(2)}) copy-start(bf16[512,1024]{1,0:T(8,128)(2,1)} %w_o.1) | copy-start | bytes 3145732
  6.6 1.2 %copy-start.4 = (bf16[1024,512]{1,0:T(8,128)(2,1)S(1)}, bf16[1024,512]{1,0:T(8,128)(2,1)}, u32[]{:S(2)}) copy-start(bf16[1024,512]{1,0:T(8,128)(2,1)} %p_q.1) | copy-start | bytes 3145732
  7.8 0.9 %copy-start.5 = (bf16[128,1024]{1,0:T(8,128)(2,1)S(1)}, bf16[128,1024]{1,0:T(8,128)(2,1)}, u32[]{:S(2)}) copy-start(bf16[128,1024]{1,0:T(8,128)(2,1)} %mesh_state.1) | copy-start | bytes 786436
  8.7 0.9 %copy-start.6 = (bf16[100,1024]{1,0:T(8,128)(2,1)S(1)}, bf16[100,1024]{1,0:T(8,128)(2,1)}, u32[]{:S(2)}) copy-start(bf16[100,1024]{1,0:T(8,128)(2,1)} %w_embed.1) | copy-start | bytes 614404

commit v2 on v1

--- a/solution.py
+++ b/solution.py
@@ -1,4 +1,3 @@
-import functools
 import math
 
 import jax
@@ -56,7 +55,7 @@
     twin = {"nodes": region, "heads": 1 - core}
     ch, half = fields.shape
     nodes, width = mesh_state.shape
-    fan = senders.shape[1]
+    fan = senders.shape[0]
     cols = w_q.shape[1]
     pairs = cols // LANES
     cap = send_rows.shape[2]
@@ -89,7 +88,7 @@
 
     def loaded(*targets):
         for target in targets:
-            loads[id(target)].wait()
+            loads.pop(id(target)).wait()
 
     loaded(own_v, rows_v)
     widen = (iota((LANES, ch), 0) == iota((LANES, ch), 1)).astype(BF16)
@@ -135,21 +134,16 @@
         target[1] = low
 
     loaded(send_v, mask_v)
-    block = 32
-    place = iota((1, points), 1)
-    place = jnp.where(place < half, place + core * half, place - core * half)
-    place = jnp.concatenate([place, iota((1, remote), 1) + points], axis=1)
-
-    def count(step, carry):
-        part = pl.ds(pl.multiple_of(step * block, block), block)
-        live = jnp.where(mask_v[part, :] > 0, send_v[part, :], -1)
-        total = jnp.zeros((block, points + remote), F32)
+    live = jnp.where(mask_v[...] > 0, send_v[...], -1)
+    for step in range((points + remote) // LANES):
+        start = step * LANES
+        if start < points:
+            start = lax.rem(start + core * half, points)
+        total = jnp.zeros((LANES, nodes), F32)
         for slot in range(fan):
-            total += (live[:, slot : slot + 1] == place).astype(F32)
-        bias[part, :] = jnp.where(total > 0, jnp.log2(jnp.maximum(total, 1.0)), -1e30)
-        return carry
-
-    lax.fori_loop(0, nodes // block, count, 0)
+            total += (live[slot : slot + 1, :] - start == iota((LANES, nodes), 0)).astype(F32)
+        total = jnp.where(total > 0, jnp.log2(jnp.maximum(total, 1.0)), -1e30)
+        bias[:, step * LANES : (step + 1) * LANES] = total.T
 
     loaded(mesh_v, wq_v)
     normed = normalize(mesh_v[...].astype(F32)).astype(BF16)
@@ -249,8 +243,9 @@
 
 
 def local(*args):
+    args = args[:12] + (args[12].T, args[13].T)
     fields, mesh_state = args[0], args[1]
-    send_rows, senders = args[11], args[12]
+    send_rows = args[11]
     ch, half = fields.shape
     nodes, width = mesh_state.shape
     cols = args[3].shape[1]
@@ -286,11 +281,11 @@
     return pl.pallas_call(
         kernel,
         out_shape=jax.ShapeDtypeStruct((nodes // 2, width), BF16),
-        in_specs=[pl.BlockSpec(memory_space=pl.ANY)] * len(args),
+        in_specs=[pl.BlockSpec(memory_space=pltpu.HBM)] * len(args),
         out_specs=pl.BlockSpec(memory_space=pltpu.VMEM),
         scratch_shapes=copies + buffers + semaphores,
         compiler_params=pltpu.CompilerParams(
-            collective_id=0, has_side_effects=True, vmem_limit_bytes=48 * 1024 * 1024
+            collective_id=0, has_side_effects=True, vmem_limit_bytes=56 * 1024 * 1024
         ),
         cost_estimate=pl.CostEstimate(
             flops=3_000_000_000, bytes_accessed=9_500_000, transcendentals=800_000

time: 38.9 us -> 30.5 us (0.78); the launches traced: 38.4 us -> 30.4 us
  local copies, waits for them, and re-layouts: 10.3 us -> 1.57 us
  Pallas kernels: 28.1 us -> 28.8 us
    unnamed x23 -> x1, local copies, waits for them, and re-layouts: 10.3 us -> 1.57 us
    pallas_call x1, Pallas kernels: 28.1 us -> 28.8 us  [local(): pl.pallas_call(kernel, out_shape=jax.ShapeDtypeStruct((nodes // 2, width)...]
where the time goes in v2:
time: 30.5 us; the launch traced here: 30.4 us
  Pallas kernels  28.8 us (94%)
  local copies, waits for them, and re-layouts  1.57 us (5%)
    pallas_call x1, Pallas kernels, local(): pl.pallas_call(kernel, out_shape=jax.ShapeDtypeStruct((nodes // 2, width)...  28.8 us
    unnamed x1, local copies, waits for them, and re-layouts  1.57 us

profile of v2, /device:TPU:1, one launch (start us, length us, event | category | flops | bytes accessed | tf_op | source)
XLA Modules:
  0.0 30.4 jit_solution(16218133020624199929)
XLA Ops:
  0.0 28.8 %encode_and_process.1 = bf16[64,1024]{1,0:T(8,128)(2,1)} custom-call(bf16[100,256]{1,0:T(8,128)(2,1)} %fields.1, bf16[128,1024]{1,0:T(8,128)(2,1)} %mesh_state.1, bf16[100,1024]{1,0:T(8,128)(2,1)} %w_embed.1, bf16[1024,512]{1,0:T(8,128)(2,1)} %w_q.1, bf16[1024,512]{1,0:T(8,128)(2,1)} %w_k.1, bf16[1024,512]{1,0:T(8,128)(2,1)} %w_v.1, bf16[512,1024]{1,0:T(8,128)(2,1)} %w_o.1, ...), custom_call_target="tpu_custom_call" | custom-call | flops 3000000000 | bytes 9500000 | tf_op jit(solution)/shard_map/encode_and_process/pallas_call | solution.py:281
  28.8 1.6 %copy.16 = bf16[64,1024]{1,0:T(8,128)(2,1)} copy(bf16[64,1024]{1,0:T(8,128)(2,1)} %encode_and_process.1) | data formatting | bytes 262144

commit v3 on v2

v3 whole, which is shorter than its diff:
```python
import functools
import math

import jax
import jax.numpy as jnp
from jax import lax
from jax.experimental import pallas as pl
from jax.experimental.pallas import tpu as pltpu
from jax.sharding import PartitionSpec as P

HEADS = 16
HS = 64
NEIGH = 4
STEPS = 4
F32 = jnp.float32
BF16 = jnp.bfloat16
MESH = pl.DeviceIdType.MESH
LANES = 128
LOG2E = math.log2(math.e)
NN = (((1,), (0,)), ((), ()))
NT = (((1,), (1,)), ((), ()))


def offset_of(slot):
    return (slot // 2 + 1) * (1 if slot % 2 == 0 else -1)


def dot(a, b, dims=NN):
    return lax.dot_general(a, b, dims, preferred_element_type=F32)


def split(x):
    high = x.astype(BF16)
    return high, (x - high.astype(F32)).astype(BF16)


def normalize(x):
    centred = x - jnp.mean(x, axis=-1, keepdims=True)
    spread = jnp.mean(centred * centred, axis=-1, keepdims=True)
    return centred * lax.rsqrt(spread + 1e-05)


def iota(shape, axis):
    return lax.broadcasted_iota(jnp.int32, shape, axis)


def kernel(
    fields, mesh_state, w_embed, w_q, w_k, w_v, w_o, p_q, p_k, p_v, p_o, send_rows, senders, mask,
    out,
    own_v, mesh_v, embed_v, wq_v, wk_v, wv_v, wo_v, pq_v, pk_v, pv_v, po_v, rows_v, send_v, mask_v,
    other_v, listed, received, table, last, values, bias, queries, hidden, sums_out, sums_in,
    context, tail, last_out, last_in,
    load_sem, half_sem, list_send, list_recv, sum_send, sum_recv, last_send, last_recv,
    wrap_sem,
):
    n = lax.axis_size("nodes")
    region, core = lax.axis_index("nodes"), lax.axis_index("heads")
    twin = {"nodes": region, "heads": 1 - core}
    ch, half = fields.shape
    nodes, width = mesh_state.shape
    fan = senders.shape[0]
    cols = w_q.shape[1]
    pairs = cols // LANES
    cap = send_rows.shape[2]
    points = 2 * half
    remote = NEIGH * cap
    own_rows = nodes // 2
    steps = sums_out.shape[0]
    chunk = width // steps
    exponent = LOG2E / math.sqrt(HS)

    def neighbour(slot, other):
        place = lax.rem(region + (offset_of(slot) + n), n)
        return {"nodes": place, "heads": 1 - core if other else core}

    loads = {}
    pieces = [
        (fields, own_v), (send_rows, rows_v), (w_embed, embed_v), (senders, send_v), (mask, mask_v),
        (mesh_state, mesh_v), (w_q, wq_v), (w_k, wk_v), (w_v, wv_v), (w_o, wo_v),
        (p_q, pq_v), (p_k, pk_v), (p_v, pv_v), (p_o, po_v),
    ]
    for index, (source, target) in enumerate(pieces):
        loads[id(target)] = pltpu.make_async_copy(source, target, load_sem.at[index])

    def loaded(*targets):
        for target in targets:
            loads.pop(id(target)).wait()

    for _, target in pieces[:3]:
        loads[id(target)].start()
    barrier = pltpu.get_barrier_semaphore()

    def greet(slot, semaphore):
        for other in range(2):
            pl.semaphore_signal(
                semaphore, inc=1, device_id=neighbour(slot, other), device_id_type=MESH
            )

    pl.semaphore_signal(barrier, inc=1, device_id=twin, device_id_type=MESH)
    for slot in range(NEIGH):
        if offset_of(slot) < 0:
            greet(slot, barrier)
        else:
            pl.when(region + offset_of(slot) < n)(functools.partial(greet, slot, barrier))
    late = sum((region + offset_of(slot) < 0).astype(jnp.int32) for slot in range(NEIGH))
    for _, target in pieces[3:]:
        loads[id(target)].start()

    loaded(own_v, rows_v)
    widen = (iota((LANES, ch), 0) == iota((LANES, ch), 1)).astype(BF16)
    own = dot(widen, own_v[...]).astype(BF16)
    rows = rows_v[0]
    wanted = jnp.concatenate([rows[j : j + 1, :] for j in range(NEIGH)], axis=1) - core * half
    pick = (iota((half, remote), 0) == wanted).astype(BF16)
    listed[...] = dot(own, pick).T.astype(BF16)

    pl.semaphore_wait(barrier, 1 + 2 * NEIGH - 2 * late)
    def list_copies(slot):
        part = pl.ds(slot * cap, cap)
        return [
            pltpu.make_async_remote_copy(
                src_ref=listed.at[part], dst_ref=received.at[other, part],
                send_sem=list_send.at[2 * slot + other], recv_sem=list_recv.at[2 * slot + other],
                device_id=neighbour(slot, other), device_id_type=MESH,
            )
            for other in range(2)
        ]

    def send_list(slot):
        for copy in list_copies(slot):
            copy.start()

    ahead = [slot for slot in range(NEIGH) if offset_of(slot) > 0]
    behind = [slot for slot in range(NEIGH) if offset_of(slot) < 0]
    for slot in ahead:
        send_list(slot)
    for slot in ahead:
        pl.when(region + offset_of(slot) >= n)(functools.partial(greet, slot, wrap_sem))
    for slot in behind:
        pl.when(region + offset_of(slot) >= 0)(functools.partial(send_list, slot))
    half_copy = pltpu.make_async_remote_copy(
        src_ref=fields, dst_ref=other_v, send_sem=half_sem.at[0], recv_sem=half_sem.at[1],
        device_id=twin, device_id_type=MESH,
    )
    half_copy.start()

    loaded(embed_v)
    embed = dot(widen, embed_v[...])
    embed = jnp.where(iota((LANES, 1), 0) == ch, 1.0, embed).astype(BF16)
    gram = dot(embed, embed, NT) * (1.0 / width)
    mean = gram[:, ch : ch + 1]
    gram = jnp.concatenate(split(gram - mean * gram[ch : ch + 1, :]), axis=1)

    def through(weight):
        both = dot(embed, weight[...])
        return split(both - mean * both[ch : ch + 1, :])

    def inverse_of(squares, axis):
        squares = jnp.maximum(jnp.sum(squares, axis=axis, keepdims=True), 0.0)
        return lax.rsqrt(squares + 1e-05)

    def place_half(block, first):
        twice = jnp.concatenate([block, block], axis=0)
        table[:, first : first + half] = twice
        block = block.astype(F32)
        squares = dot(gram, twice) * block
        last[first : first + half, :] = block.T.astype(BF16)
        return inverse_of(squares, 0), inverse_of(squares.T, 1)

    inverse, scale = place_half(own, 0)

    loaded(send_v, mask_v)
    spot = send_v[...]
    tiles = (points + remote) // LANES
    word = jnp.zeros_like(spot)
    for tile in range(tiles):
        word = jnp.where(spot >= tile * LANES, 1 << (6 * tile), word)
    word = jnp.where(mask_v[...] > 0, word, 0)
    spot = spot & (LANES - 1)
    down = iota((LANES, nodes), 0)
    counts = jnp.zeros((LANES, nodes), jnp.int32)
    for slot in range(fan):
        counts += jnp.where(spot[slot : slot + 1, :] == down, word[slot : slot + 1, :], 0)
    counts = counts.T
    for tile in range(tiles):
        total = ((counts >> (6 * tile)) & 63).astype(F32)
        total = jnp.where(total > 0, jnp.log2(jnp.maximum(total, 1.0)), -1e30)
        first = tile * LANES
        if first < points:
            first = lax.rem(first + core * half, points)
        bias[:, pl.ds(pl.multiple_of(first, LANES), LANES)] = total

    loaded(mesh_v, wq_v)
    normed = normalize(mesh_v[...].astype(F32)).astype(BF16)
    enc_queries = dot(normed, wq_v[...]).astype(BF16)

    loaded(wk_v)
    k_high, k_low = through(wk_v)
    low_lanes = iota((nodes, LANES), 1) < HS

    def lanes_of(pair):
        return slice(pair * LANES, (pair + 1) * LANES)

    def two_heads(rows):
        zeros = jnp.zeros_like(rows)
        even, odd = jnp.where(low_lanes, rows, zeros), jnp.where(low_lanes, zeros, rows)
        return jnp.concatenate([even, odd], axis=0)

    for pair in range(pairs):
        lanes = lanes_of(pair)
        two = two_heads(enc_queries[:, lanes])
        keys = jnp.concatenate([k_high[:, lanes], k_low[:, lanes]], axis=1)
        high, low = split(dot(jnp.concatenate([two, two], axis=1), keys, NT))
        queries[pair, :, 0:LANES] = high
        queries[pair, :, LANES : 2 * LANES] = low

    loaded(wv_v)
    v_both = jnp.concatenate(through(wv_v), axis=0)

    def values_of(rows, scale):
        return (dot(jnp.concatenate([rows, rows], axis=1), v_both) * scale).astype(BF16)

    def weigh(logits, edges, inverse):
        logits = logits * (inverse * exponent) + jnp.concatenate([edges, edges], axis=0)
        top = jnp.max(logits, axis=-1, keepdims=True)
        return top, jnp.exp2(logits - top).astype(BF16)

    def join_heads(rows):
        return jnp.where(low_lanes, rows[:nodes], rows[nodes:])

    def mix(probs, values):
        mixed = dot(probs, jnp.concatenate([values, jnp.ones_like(values)], axis=1))
        return join_heads(mixed[:, :LANES]), join_heads(mixed[:, LANES:])

    half_copy.wait()
    other_inverse, other_scale = place_half(dot(widen, other_v[...]).astype(BF16), half)
    inverse = jnp.concatenate([inverse, other_inverse], axis=1)
    values[0:half, :] = values_of(last[0:half, :], scale)
    values[half:points, :] = values_of(last[half:points, :], other_scale)
    near = []
    for pair in range(pairs):
        logits = dot(queries[pair], table[...])
        top, probs = weigh(logits, bias[:, 0:points], inverse)
        near.append((top, *mix(probs, values[:, lanes_of(pair)])))

    loaded(wo_v)
    pl.when(late > 0)(lambda: pl.semaphore_wait(wrap_sem, 2 * late))
    for slot in behind:
        pl.when(region + offset_of(slot) < 0)(functools.partial(send_list, slot))
    for slot in range(NEIGH):
        for copy in list_copies(slot):
            copy.wait()
    far = received[0] + received[1]
    far_twice = jnp.concatenate([far, far], axis=1)
    squares = dot(far_twice, gram, NT) * far.astype(F32)
    inverse = inverse_of(squares.T, 0)
    far_values = values_of(far, inverse_of(squares, 1))
    for pair in range(pairs):
        lanes = lanes_of(pair)
        logits = dot(queries[pair], far_twice, NT)
        top, probs = weigh(logits, bias[:, points : points + remote], inverse)
        mixed, total = mix(probs, far_values[:, lanes])
        near_top, near_mixed, near_total = near[pair]
        best = jnp.maximum(top, near_top)
        gain = join_heads(jnp.exp2(top - best))
        near_gain = join_heads(jnp.exp2(near_top - best))
        both = gain * mixed + near_gain * near_mixed
        context[:, lanes] = (both / (gain * total + near_gain * near_total)).astype(BF16)

    sum_copies = []
    for step in range(steps):
        lanes = slice(step * chunk, (step + 1) * chunk)
        part = dot(context[...], wo_v[:, lanes])
        sums_out[step] = part.astype(BF16)
        sum_copies.append(
            pltpu.make_async_remote_copy(
                src_ref=sums_out.at[step], dst_ref=sums_in.at[step],
                send_sem=sum_send.at[step], recv_sem=sum_recv.at[step],
                device_id=twin, device_id_type=MESH,
            )
        )
        sum_copies[-1].start()
        hidden[:, lanes] = mesh_v[:, lanes].astype(F32) + part
    loaded(pq_v, pk_v, pv_v, po_v)
    for step in range(steps):
        lanes = slice(step * chunk, (step + 1) * chunk)
        sum_copies[step].wait()
        hidden[:, lanes] += sums_in[step].astype(F32)

    normed = normalize(hidden[...]).astype(BF16)
    proc_q = dot(normed, pq_v[...]).astype(BF16)
    proc_k = dot(normed, pk_v[...]).astype(BF16)
    proc_v = dot(normed, pv_v[...]).astype(BF16)
    for pair in range(pairs):
        lanes = lanes_of(pair)
        logits = dot(two_heads(proc_q[:, lanes]), proc_k[:, lanes], NT) * exponent
        probs = jnp.exp2(logits - jnp.max(logits, axis=-1, keepdims=True)).astype(BF16)
        mixed, total = mix(probs, proc_v[:, lanes])
        context[:, lanes] = (mixed / total).astype(BF16)

    theirs = pl.ds(pl.multiple_of((1 - core) * own_rows, own_rows), own_rows)
    mine = pl.ds(pl.multiple_of(core * own_rows, own_rows), own_rows)
    last_copies = []
    for step in range(steps):
        lanes = slice(step * chunk, (step + 1) * chunk)
        tail[:, lanes] = dot(context[...], po_v[:, lanes])
        last_out[step] = tail[theirs, lanes].astype(BF16)
        last_copies.append(
            pltpu.make_async_remote_copy(
                src_ref=last_out.at[step], dst_ref=last_in.at[step],
                send_sem=last_send.at[step], recv_sem=last_recv.at[step],
                device_id=twin, device_id_type=MESH,
            )
        )
        last_copies[-1].start()
    for step in range(steps):
        lanes = slice(step * chunk, (step + 1) * chunk)
        part = hidden[mine, lanes] + tail[mine, lanes]
        last_copies[step].wait()
        out[:, lanes] = (part + last_in[step].astype(F32)).astype(BF16)


def local(*args):
    args = args[:12] + (args[12].T, args[13].T)
    fields, mesh_state = args[0], args[1]
    send_rows = args[11]
    ch, half = fields.shape
    nodes, width = mesh_state.shape
    cols = args[3].shape[1]
    pairs = cols // LANES
    remote = send_rows.shape[1] * send_rows.shape[2]
    columns = 2 * half + remote
    copies = [pltpu.VMEM(x.shape, x.dtype) for x in args]
    buffers = [
        pltpu.VMEM((ch, half), BF16),
        pltpu.VMEM((remote, LANES), BF16),
        pltpu.VMEM((2, remote, LANES), BF16),
        pltpu.VMEM((2 * LANES, 2 * half), BF16),
        pltpu.VMEM((2 * half, LANES), BF16),
        pltpu.VMEM((2 * half, cols), BF16),
        pltpu.VMEM((nodes, columns), F32),
        pltpu.VMEM((pairs, 2 * nodes, 2 * LANES), BF16),
        pltpu.VMEM((nodes, width), F32),
        pltpu.VMEM((STEPS, nodes, width // STEPS), BF16),
        pltpu.VMEM((STEPS, nodes, width // STEPS), BF16),
        pltpu.VMEM((nodes, cols), BF16),
        pltpu.VMEM((nodes, width), F32),
        pltpu.VMEM((STEPS, nodes // 2, width // STEPS), BF16),
        pltpu.VMEM((STEPS, nodes // 2, width // STEPS), BF16),
    ]
    semaphores = [
        pltpu.SemaphoreType.DMA((len(args),)),
        pltpu.SemaphoreType.DMA((2,)),
        pltpu.SemaphoreType.DMA((2 * NEIGH,)),
        pltpu.SemaphoreType.DMA((2 * NEIGH,)),
    ] + [pltpu.SemaphoreType.DMA((STEPS,))] * 4 + [pltpu.SemaphoreType.REGULAR]
    return pl.pallas_call(
        kernel,
        out_shape=jax.ShapeDtypeStruct((nodes // 2, width), BF16),
        in_specs=[pl.BlockSpec(memory_space=pltpu.HBM)] * len(args),
        out_specs=pl.BlockSpec(memory_space=pltpu.VMEM),
        scratch_shapes=copies + buffers + semaphores,
        compiler_params=pltpu.CompilerParams(
            collective_id=0, has_side_effects=True, vmem_limit_bytes=56 * 1024 * 1024
        ),
        cost_estimate=pl.CostEstimate(
            flops=3_000_000_000, bytes_accessed=9_500_000, transcendentals=800_000
        ),
        name="encode_and_process",
    )(*args)


def solution(mesh):
    return jax.shard_map(
        local,
        mesh=mesh,
        in_specs=(
            P(None, ("nodes", "heads")),
            P("nodes", None),
            P(),
            P(None, "heads"),
            P(None, "heads"),
            P(None, "heads"),
            P("heads", None),
            P(None, "heads"),
            P(None, "heads"),
            P(None, "heads"),
            P("heads", None),
            P("nodes", None, None),
            P("nodes", None),
            P("nodes", None),
        ),
        out_specs=P(("nodes", "heads"), None),
        check_vma=False,
    )
```

time: 30.5 us -> 27.8 us (0.911)
  Pallas kernels: 28.8 us -> 26.1 us
    pallas_call x1, Pallas kernels: 28.8 us -> 26.1 us  [local(): pl.pallas_call(kernel, out_shape=jax.ShapeDtypeStruct((nodes // 2, width)...]
where the time goes in v3:
time: 27.8 us; the launch traced here: 27.7 us
  Pallas kernels  26.1 us (94%)
  local copies, waits for them, and re-layouts  1.57 us (6%)
    pallas_call x1, Pallas kernels, local(): pl.pallas_call(kernel, out_shape=jax.ShapeDtypeStruct((nodes // 2, width)...  26.1 us
    unnamed x1, local copies, waits for them, and re-layouts  1.57 us

profile of v3, /device:TPU:1, one launch (start us, length us, event | category | flops | bytes accessed | tf_op | source)
XLA Modules:
  0.0 27.7 jit_solution(15422815423839988381)
XLA Ops:
  0.0 26.1 %encode_and_process.1 = bf16[64,1024]{1,0:T(8,128)(2,1)} custom-call(bf16[100,256]{1,0:T(8,128)(2,1)} %fields.1, bf16[128,1024]{1,0:T(8,128)(2,1)} %mesh_state.1, bf16[100,1024]{1,0:T(8,128)(2,1)} %w_embed.1, bf16[1024,512]{1,0:T(8,128)(2,1)} %w_q.1, bf16[1024,512]{1,0:T(8,128)(2,1)} %w_k.1, bf16[1024,512]{1,0:T(8,128)(2,1)} %w_v.1, bf16[512,1024]{1,0:T(8,128)(2,1)} %w_o.1, ...), custom_call_target="tpu_custom_call" | custom-call | flops 3000000000 | bytes 9500000 | tf_op jit(solution)/shard_map/encode_and_process/pallas_call | solution.py:357
  26.1 1.6 %copy.16 = bf16[64,1024]{1,0:T(8,128)(2,1)} copy(bf16[64,1024]{1,0:T(8,128)(2,1)} %encode_and_process.1) | data formatting | bytes 262144

commit v4 on v3

--- a/solution.py
+++ b/solution.py
@@ -11,7 +11,7 @@
 HEADS = 16
 HS = 64
 NEIGH = 4
-STEPS = 4
+STEPS = 2
 F32 = jnp.float32
 BF16 = jnp.bfloat16
 MESH = pl.DeviceIdType.MESH
@@ -201,6 +201,9 @@
     def lanes_of(pair):
         return slice(pair * LANES, (pair + 1) * LANES)
 
+    def rows_of(pair):
+        return slice(2 * pair * nodes, 2 * (pair + 1) * nodes)
+
     def two_heads(rows):
         zeros = jnp.zeros_like(rows)
         even, odd = jnp.where(low_lanes, rows, zeros), jnp.where(low_lanes, zeros, rows)
@@ -211,8 +214,8 @@
         two = two_heads(enc_queries[:, lanes])
         keys = jnp.concatenate([k_high[:, lanes], k_low[:, lanes]], axis=1)
         high, low = split(dot(jnp.concatenate([two, two], axis=1), keys, NT))
-        queries[pair, :, 0:LANES] = high
-        queries[pair, :, LANES : 2 * LANES] = low
+        queries[rows_of(pair), 0:LANES] = high
+        queries[rows_of(pair), LANES : 2 * LANES] = low
 
     loaded(wv_v)
     v_both = jnp.concatenate(through(wv_v), axis=0)
@@ -232,16 +235,16 @@
         mixed = dot(probs, jnp.concatenate([values, jnp.ones_like(values)], axis=1))
         return join_heads(mixed[:, :LANES]), join_heads(mixed[:, LANES:])
 
-    half_copy.wait()
+    half_copy.wait_recv()
     other_inverse, other_scale = place_half(dot(widen, other_v[...]).astype(BF16), half)
     inverse = jnp.concatenate([inverse, other_inverse], axis=1)
     values[0:half, :] = values_of(last[0:half, :], scale)
     values[half:points, :] = values_of(last[half:points, :], other_scale)
     near = []
     for pair in range(pairs):
-        logits = dot(queries[pair], table[...])
+        logits = dot(queries[rows_of(pair), :], table[...])
         top, probs = weigh(logits, bias[:, 0:points], inverse)
-        near.append((top, *mix(probs, values[:, lanes_of(pair)])))
+        near.append((join_heads(top), *mix(probs, values[:, lanes_of(pair)])))
 
     loaded(wo_v)
     pl.when(late > 0)(lambda: pl.semaphore_wait(wrap_sem, 2 * late))
@@ -249,21 +252,30 @@
         pl.when(region + offset_of(slot) < 0)(functools.partial(send_list, slot))
     for slot in range(NEIGH):
         for copy in list_copies(slot):
-            copy.wait()
+            copy.wait_recv()
     far = received[0] + received[1]
     far_twice = jnp.concatenate([far, far], axis=1)
     squares = dot(far_twice, gram, NT) * far.astype(F32)
     inverse = inverse_of(squares.T, 0)
+    far_down = far.astype(F32).T.astype(BF16)
+    far_down = jnp.concatenate([far_down, far_down], axis=0)
+    middle = pairs * nodes
+    far_logits = jnp.concatenate(
+        [dot(queries[0:middle, :], far_down), dot(queries[middle : 2 * middle, :], far_down)], axis=0
+    )
+    far_weights = [
+        weigh(far_logits[rows_of(pair)], bias[:, points : points + remote], inverse)
+        for pair in range(pairs)
+    ]
     far_values = values_of(far, inverse_of(squares, 1))
     for pair in range(pairs):
         lanes = lanes_of(pair)
-        logits = dot(queries[pair], far_twice, NT)
-        top, probs = weigh(logits, bias[:, points : points + remote], inverse)
+        top, probs = far_weights[pair]
         mixed, total = mix(probs, far_values[:, lanes])
         near_top, near_mixed, near_total = near[pair]
+        top = join_heads(top)
         best = jnp.maximum(top, near_top)
-        gain = join_heads(jnp.exp2(top - best))
-        near_gain = join_heads(jnp.exp2(near_top - best))
+        gain, near_gain = jnp.exp2(top - best), jnp.exp2(near_top - best)
         both = gain * mixed + near_gain * near_mixed
         context[:, lanes] = (both / (gain * total + near_gain * near_total)).astype(BF16)
 
@@ -284,18 +296,21 @@
     loaded(pq_v, pk_v, pv_v, po_v)
     for step in range(steps):
         lanes = slice(step * chunk, (step + 1) * chunk)
-        sum_copies[step].wait()
+        sum_copies[step].wait_recv()
         hidden[:, lanes] += sums_in[step].astype(F32)
 
     normed = normalize(hidden[...]).astype(BF16)
     proc_q = dot(normed, pq_v[...]).astype(BF16)
     proc_k = dot(normed, pk_v[...]).astype(BF16)
+    probs = []
+    for pair in range(pairs):
+        lanes = lanes_of(pair)
+        logits = dot(two_heads(proc_q[:, lanes]), proc_k[:, lanes], NT) * exponent
+        probs.append(jnp.exp2(logits - jnp.max(logits, axis=-1, keepdims=True)).astype(BF16))
     proc_v = dot(normed, pv_v[...]).astype(BF16)
     for pair in range(pairs):
         lanes = lanes_of(pair)
-        logits = dot(two_heads(proc_q[:, lanes]), proc_k[:, lanes], NT) * exponent
-        probs = jnp.exp2(logits - jnp.max(logits, axis=-1, keepdims=True)).astype(BF16)
-        mixed, total = mix(probs, proc_v[:, lanes])
+        mixed, total = mix(probs[pair], proc_v[:, lanes])
         context[:, lanes] = (mixed / total).astype(BF16)
 
     theirs = pl.ds(pl.multiple_of((1 - core) * own_rows, own_rows), own_rows)
@@ -316,8 +331,13 @@
     for step in range(steps):
         lanes = slice(step * chunk, (step + 1) * chunk)
         part = hidden[mine, lanes] + tail[mine, lanes]
-        last_copies[step].wait()
+        last_copies[step].wait_recv()
         out[:, lanes] = (part + last_in[step].astype(F32)).astype(BF16)
+    for copy in [half_copy, *sum_copies, *last_copies]:
+        copy.wait_send()
+    for slot in range(NEIGH):
+        for copy in list_copies(slot):
+            copy.wait_send()
 
 
 def local(*args):
@@ -339,7 +359,7 @@
         pltpu.VMEM((2 * half, LANES), BF16),
         pltpu.VMEM((2 * half, cols), BF16),
         pltpu.VMEM((nodes, columns), F32),
-        pltpu.VMEM((pairs, 2 * nodes, 2 * LANES), BF16),
+        pltpu.VMEM((pairs * 2 * nodes, 2 * LANES), BF16),
         pltpu.VMEM((nodes, width), F32),
         pltpu.VMEM((STEPS, nodes, width // STEPS), BF16),
         pltpu.VMEM((STEPS, nodes, width // STEPS), BF16),
@@ -356,7 +376,7 @@
     ] + [pltpu.SemaphoreType.DMA((STEPS,))] * 4 + [pltpu.SemaphoreType.REGULAR]
     return pl.pallas_call(
         kernel,
-        out_shape=jax.ShapeDtypeStruct((nodes // 2, width), BF16),
+        out_shape=pltpu.VMEM((nodes // 2, width), BF16),
         in_specs=[pl.BlockSpec(memory_space=pltpu.HBM)] * len(args),
         out_specs=pl.BlockSpec(memory_space=pltpu.VMEM),
         scratch_shapes=copies + buffers + semaphores,

time: 27.8 us -> 25.3 us (0.910)
  Pallas kernels: 26.1 us -> 24.5 us
  local copies, waits for them, and re-layouts: 1.57 us -> 0.66 us
    pallas_call x1, Pallas kernels: 26.1 us -> 24.5 us  [local(): pl.pallas_call(kernel, out_shape=pltpu.VMEM((nodes // 2, width), BF16), i...]
    unnamed x1, local copies, waits for them, and re-layouts: 1.57 us -> 0.66 us
where the time goes in v4:
time: 25.3 us; the launch traced here: 25.2 us
  Pallas kernels  24.5 us (97%)
  local copies, waits for them, and re-layouts  0.66 us (3%)
    pallas_call x1, Pallas kernels, local(): pl.pallas_call(kernel, out_shape=pltpu.VMEM((nodes // 2, width), BF16), i...  24.5 us
    unnamed x1, local copies, waits for them, and re-layouts  0.66 us

profile of v4, /device:TPU:1, one launch (start us, length us, event | category | flops | bytes accessed | tf_op | source)
XLA Modules:
  0.0 25.2 jit_solution(1673451754204251199)
XLA Ops:
  0.0 24.5 %encode_and_process.1 = bf16[64,1024]{1,0:T(8,128)(2,1)S(1)} custom-call(bf16[100,256]{1,0:T(8,128)(2,1)} %fields.1, bf16[128,1024]{1,0:T(8,128)(2,1)} %mesh_state.1, bf16[100,1024]{1,0:T(8,128)(2,1)} %w_embed.1, bf16[1024,512]{1,0:T(8,128)(2,1)} %w_q.1, bf16[1024,512]{1,0:T(8,128)(2,1)} %w_k.1, bf16[1024,512]{1,0:T(8,128)(2,1)} %w_v.1, ...), custom_call_target="tpu_custom_call" | custom-call | flops 3000000000 | bytes 9500000 | tf_op jit(solution)/shard_map/encode_and_process/pallas_call | solution.py:377
  24.5 0.7 %copy.16 = bf16[64,1024]{1,0:T(8,128)(2,1)} copy(bf16[64,1024]{1,0:T(8,128)(2,1)S(1)} %encode_and_process.1) | data formatting | bytes 262144

commit v5 on v4

--- a/solution.py
+++ b/solution.py
@@ -48,9 +48,9 @@
     fields, mesh_state, w_embed, w_q, w_k, w_v, w_o, p_q, p_k, p_v, p_o, send_rows, senders, mask,
     out,
     own_v, mesh_v, embed_v, wq_v, wk_v, wv_v, wo_v, pq_v, pk_v, pv_v, po_v, rows_v, send_v, mask_v,
-    other_v, listed, received, table, last, values, bias, queries, hidden, sums_out, sums_in,
-    context, tail, last_out, last_in,
-    load_sem, half_sem, list_send, list_recv, sum_send, sum_recv, last_send, last_recv,
+    other_v, listed, received, table, last, values, bias, queries, hidden,     context, tail, last_out, last_in, w_other, w_joint, context_in, ahead_sum,
+    context_late,
+    load_sem, half_sem, list_send, list_recv, weight_sem, sum_send, sum_recv, last_send, last_recv,
     wrap_sem,
 ):
     n = lax.axis_size("nodes")
@@ -65,7 +65,7 @@
     points = 2 * half
     remote = NEIGH * cap
     own_rows = nodes // 2
-    steps = sums_out.shape[0]
+    steps = last_out.shape[0]
     chunk = width // steps
     exponent = LOG2E / math.sqrt(HS)
 
@@ -143,13 +143,20 @@
         device_id=twin, device_id_type=MESH,
     )
     half_copy.start()
+    weight_copy = pltpu.make_async_remote_copy(
+        src_ref=w_o, dst_ref=w_other, send_sem=weight_sem.at[0], recv_sem=weight_sem.at[1],
+        device_id=twin, device_id_type=MESH,
+    )
+    weight_copy.start()
 
     loaded(embed_v)
     embed = dot(widen, embed_v[...])
     embed = jnp.where(iota((LANES, 1), 0) == ch, 1.0, embed).astype(BF16)
     gram = dot(embed, embed, NT) * (1.0 / width)
     mean = gram[:, ch : ch + 1]
-    gram = jnp.concatenate(split(gram - mean * gram[ch : ch + 1, :]), axis=1)
+    gram = split(gram - mean * gram[ch : ch + 1, :])
+    gram_down = jnp.concatenate(gram, axis=0)
+    gram = jnp.concatenate(gram, axis=1)
 
     def through(weight):
         both = dot(embed, weight[...])
@@ -246,6 +253,14 @@
         top, probs = weigh(logits, bias[:, 0:points], inverse)
         near.append((join_heads(top), *mix(probs, values[:, lanes_of(pair)])))
 
+    loaded(pq_v, pk_v, pv_v, po_v)
+    weight_copy.wait_recv()
+    processor = (pq_v, pk_v, pv_v)
+    sums = []
+    for index, weight in enumerate(processor):
+        w_joint[index] = dot(w_other[...], weight[...]).astype(BF16)
+        sums.append(dot(jnp.ones((8, width), BF16), weight[...])[0:1])
+
     loaded(wo_v)
     pl.when(late > 0)(lambda: pl.semaphore_wait(wrap_sem, 2 * late))
     for slot in behind:
@@ -255,13 +270,11 @@
             copy.wait_recv()
     far = received[0] + received[1]
     far_twice = jnp.concatenate([far, far], axis=1)
-    squares = dot(far_twice, gram, NT) * far.astype(F32)
+    squares = dot(far_twice, gram_down) * far.astype(F32)
     inverse = inverse_of(squares.T, 0)
-    far_down = far.astype(F32).T.astype(BF16)
-    far_down = jnp.concatenate([far_down, far_down], axis=0)
     middle = pairs * nodes
     far_logits = jnp.concatenate(
-        [dot(queries[0:middle, :], far_down), dot(queries[middle : 2 * middle, :], far_down)], axis=0
+        [dot(queries[0:middle, :], far_twice, NT), dot(queries[middle:, :], far_twice, NT)], axis=0
     )
     far_weights = [
         weigh(far_logits[rows_of(pair)], bias[:, points : points + remote], inverse)
@@ -279,46 +292,50 @@
         both = gain * mixed + near_gain * near_mixed
         context[:, lanes] = (both / (gain * total + near_gain * near_total)).astype(BF16)
 
-    sum_copies = []
-    for step in range(steps):
-        lanes = slice(step * chunk, (step + 1) * chunk)
-        part = dot(context[...], wo_v[:, lanes])
-        sums_out[step] = part.astype(BF16)
-        sum_copies.append(
-            pltpu.make_async_remote_copy(
-                src_ref=sums_out.at[step], dst_ref=sums_in.at[step],
-                send_sem=sum_send.at[step], recv_sem=sum_recv.at[step],
-                device_id=twin, device_id_type=MESH,
-            )
-        )
-        sum_copies[-1].start()
-        hidden[:, lanes] = mesh_v[:, lanes].astype(F32) + part
-    loaded(pq_v, pk_v, pv_v, po_v)
-    for step in range(steps):
-        lanes = slice(step * chunk, (step + 1) * chunk)
-        sum_copies[step].wait_recv()
-        hidden[:, lanes] += sums_in[step].astype(F32)
-
-    normed = normalize(hidden[...]).astype(BF16)
-    proc_q = dot(normed, pq_v[...]).astype(BF16)
-    proc_k = dot(normed, pk_v[...]).astype(BF16)
+    sum_copy = pltpu.make_async_remote_copy(
+        src_ref=context, dst_ref=context_in, send_sem=sum_send.at[0], recv_sem=sum_recv.at[0],
+        device_id=twin, device_id_type=MESH,
+    )
+    sum_copy.start()
+    start = mesh_v[...].astype(F32) + dot(context[...], wo_v[...])
+    shift = jnp.mean(start, axis=-1, keepdims=True)
+    start = start - shift
+    hidden[...] = start
+    start = start.astype(BF16)
+    for index, weight in enumerate(processor):
+        ahead_sum[index] = dot(start, weight[...])
+    sum_copy.wait_recv()
+
+    theirs_in = context_in[...]
+    centred = hidden[...] + dot(theirs_in, w_other[...])
+    mean = jnp.mean(centred, axis=-1, keepdims=True)
+    hidden[...] = centred + shift
+    spread = jnp.mean(centred * centred, axis=-1, keepdims=True) - mean * mean
+    rise = lax.rsqrt(jnp.maximum(spread, 0.0) + 1e-05)
+
+    raw = [ahead_sum[index] + dot(theirs_in, w_joint[index]) for index in range(3)]
+
+    def projected(index):
+        return ((raw[index] - mean * sums[index]) * rise).astype(BF16)
+
+    proc_q, proc_k = projected(0), projected(1)
     probs = []
     for pair in range(pairs):
         lanes = lanes_of(pair)
         logits = dot(two_heads(proc_q[:, lanes]), proc_k[:, lanes], NT) * exponent
         probs.append(jnp.exp2(logits - jnp.max(logits, axis=-1, keepdims=True)).astype(BF16))
-    proc_v = dot(normed, pv_v[...]).astype(BF16)
+    proc_v = projected(2)
     for pair in range(pairs):
         lanes = lanes_of(pair)
         mixed, total = mix(probs[pair], proc_v[:, lanes])
-        context[:, lanes] = (mixed / total).astype(BF16)
+        context_late[:, lanes] = (mixed / total).astype(BF16)
 
     theirs = pl.ds(pl.multiple_of((1 - core) * own_rows, own_rows), own_rows)
     mine = pl.ds(pl.multiple_of(core * own_rows, own_rows), own_rows)
     last_copies = []
     for step in range(steps):
         lanes = slice(step * chunk, (step + 1) * chunk)
-        tail[:, lanes] = dot(context[...], po_v[:, lanes])
+        tail[:, lanes] = dot(context_late[...], po_v[:, lanes])
         last_out[step] = tail[theirs, lanes].astype(BF16)
         last_copies.append(
             pltpu.make_async_remote_copy(
@@ -333,7 +350,7 @@
         part = hidden[mine, lanes] + tail[mine, lanes]
         last_copies[step].wait_recv()
         out[:, lanes] = (part + last_in[step].astype(F32)).astype(BF16)
-    for copy in [half_copy, *sum_copies, *last_copies]:
+    for copy in [half_copy, weight_copy, sum_copy, *last_copies]:
         copy.wait_send()
     for slot in range(NEIGH):
         for copy in list_copies(slot):
@@ -361,19 +378,25 @@
         pltpu.VMEM((nodes, columns), F32),
         pltpu.VMEM((pairs * 2 * nodes, 2 * LANES), BF16),
         pltpu.VMEM((nodes, width), F32),
-        pltpu.VMEM((STEPS, nodes, width // STEPS), BF16),
-        pltpu.VMEM((STEPS, nodes, width // STEPS), BF16),
         pltpu.VMEM((nodes, cols), BF16),
         pltpu.VMEM((nodes, width), F32),
         pltpu.VMEM((STEPS, nodes // 2, width // STEPS), BF16),
         pltpu.VMEM((STEPS, nodes // 2, width // STEPS), BF16),
+        pltpu.VMEM((cols, width), BF16),
+        pltpu.VMEM((3, cols, cols), BF16),
+        pltpu.VMEM((nodes, cols), BF16),
+        pltpu.VMEM((3, nodes, cols), F32),
+        pltpu.VMEM((nodes, cols), BF16),
     ]
     semaphores = [
         pltpu.SemaphoreType.DMA((len(args),)),
         pltpu.SemaphoreType.DMA((2,)),
         pltpu.SemaphoreType.DMA((2 * NEIGH,)),
         pltpu.SemaphoreType.DMA((2 * NEIGH,)),
-    ] + [pltpu.SemaphoreType.DMA((STEPS,))] * 4 + [pltpu.SemaphoreType.REGULAR]
+        pltpu.SemaphoreType.DMA((2,)),
+        pltpu.SemaphoreType.DMA((1,)),
+        pltpu.SemaphoreType.DMA((1,)),
+    ] + [pltpu.SemaphoreType.DMA((STEPS,))] * 2 + [pltpu.SemaphoreType.REGULAR]
     return pl.pallas_call(
         kernel,
         out_shape=pltpu.VMEM((nodes // 2, width), BF16),

time: 25.3 us -> 24.5 us (0.968)
  Pallas kernels: 24.5 us -> 23.8 us
    pallas_call x1, Pallas kernels: 24.5 us -> 23.8 us  [local(): pl.pallas_call(kernel, out_shape=pltpu.VMEM((nodes // 2, width), BF16), i...]
where the time goes in v5:
time: 24.5 us; the launch traced here: 24.4 us
  Pallas kernels  23.8 us (97%)
  local copies, waits for them, and re-layouts  0.66 us (3%)
    pallas_call x1, Pallas kernels, local(): pl.pallas_call(kernel, out_shape=pltpu.VMEM((nodes // 2, width), BF16), i...  23.8 us
    unnamed x1, local copies, waits for them, and re-layouts  0.66 us

profile of v5, /device:TPU:1, one launch (start us, length us, event | category | flops | bytes accessed | tf_op | source)
XLA Modules:
  0.0 24.4 jit_solution(17803331958453679887)
XLA Ops:
  0.0 23.8 %encode_and_process.1 = bf16[64,1024]{1,0:T(8,128)(2,1)S(1)} custom-call(bf16[100,256]{1,0:T(8,128)(2,1)} %fields.1, bf16[128,1024]{1,0:T(8,128)(2,1)} %mesh_state.1, bf16[100,1024]{1,0:T(8,128)(2,1)} %w_embed.1, bf16[1024,512]{1,0:T(8,128)(2,1)} %w_q.1, bf16[1024,512]{1,0:T(8,128)(2,1)} %w_k.1, bf16[1024,512]{1,0:T(8,128)(2,1)} %w_v.1, ...), custom_call_target="tpu_custom_call" | custom-call | flops 3000000000 | bytes 9500000 | tf_op jit(solution)/shard_map/encode_and_process/pallas_call | solution.py:400
  23.8 0.7 %copy.16 = bf16[64,1024]{1,0:T(8,128)(2,1)} copy(bf16[64,1024]{1,0:T(8,128)(2,1)S(1)} %encode_and_process.1) | data formatting | bytes 262144

commit v6 on v5

--- a/solution.py
+++ b/solution.py
@@ -11,7 +11,6 @@
 HEADS = 16
 HS = 64
 NEIGH = 4
-STEPS = 2
 F32 = jnp.float32
 BF16 = jnp.bfloat16
 MESH = pl.DeviceIdType.MESH
@@ -48,9 +47,9 @@
     fields, mesh_state, w_embed, w_q, w_k, w_v, w_o, p_q, p_k, p_v, p_o, send_rows, senders, mask,
     out,
     own_v, mesh_v, embed_v, wq_v, wk_v, wv_v, wo_v, pq_v, pk_v, pv_v, po_v, rows_v, send_v, mask_v,
-    other_v, listed, received, table, last, values, bias, queries, hidden,     context, tail, last_out, last_in, w_other, w_joint, context_in, ahead_sum,
+    other_v, listed, received, table, last, values, bias, queries, hidden,     context, tail, last_in, w_other, p_other, w_joint, context_in, ahead_sum,
     context_late,
-    load_sem, half_sem, list_send, list_recv, weight_sem, sum_send, sum_recv, last_send, last_recv,
+    load_sem, half_sem, list_send, list_recv, weight_send, weight_recv, sum_send, sum_recv, last_sem,
     wrap_sem,
 ):
     n = lax.axis_size("nodes")
@@ -65,8 +64,6 @@
     points = 2 * half
     remote = NEIGH * cap
     own_rows = nodes // 2
-    steps = last_out.shape[0]
-    chunk = width // steps
     exponent = LOG2E / math.sqrt(HS)
 
     def neighbour(slot, other):
@@ -143,11 +140,15 @@
         device_id=twin, device_id_type=MESH,
     )
     half_copy.start()
-    weight_copy = pltpu.make_async_remote_copy(
-        src_ref=w_o, dst_ref=w_other, send_sem=weight_sem.at[0], recv_sem=weight_sem.at[1],
-        device_id=twin, device_id_type=MESH,
-    )
-    weight_copy.start()
+    weight_copies = [
+        pltpu.make_async_remote_copy(
+            src_ref=source, dst_ref=target, send_sem=weight_send.at[index],
+            recv_sem=weight_recv.at[index], device_id=twin, device_id_type=MESH,
+        )
+        for index, (source, target) in enumerate([(w_o, w_other), (p_o, p_other)])
+    ]
+    for copy in weight_copies:
+        copy.start()
 
     loaded(embed_v)
     embed = dot(widen, embed_v[...])
@@ -254,7 +255,8 @@
         near.append((join_heads(top), *mix(probs, values[:, lanes_of(pair)])))
 
     loaded(pq_v, pk_v, pv_v, po_v)
-    weight_copy.wait_recv()
+    for copy in weight_copies:
+        copy.wait_recv()
     processor = (pq_v, pk_v, pv_v)
     sums = []
     for index, weight in enumerate(processor):
@@ -332,25 +334,15 @@
 
     theirs = pl.ds(pl.multiple_of((1 - core) * own_rows, own_rows), own_rows)
     mine = pl.ds(pl.multiple_of(core * own_rows, own_rows), own_rows)
-    last_copies = []
-    for step in range(steps):
-        lanes = slice(step * chunk, (step + 1) * chunk)
-        tail[:, lanes] = dot(context_late[...], po_v[:, lanes])
-        last_out[step] = tail[theirs, lanes].astype(BF16)
-        last_copies.append(
-            pltpu.make_async_remote_copy(
-                src_ref=last_out.at[step], dst_ref=last_in.at[step],
-                send_sem=last_send.at[step], recv_sem=last_recv.at[step],
-                device_id=twin, device_id_type=MESH,
-            )
-        )
-        last_copies[-1].start()
-    for step in range(steps):
-        lanes = slice(step * chunk, (step + 1) * chunk)
-        part = hidden[mine, lanes] + tail[mine, lanes]
-        last_copies[step].wait_recv()
-        out[:, lanes] = (part + last_in[step].astype(F32)).astype(BF16)
-    for copy in [half_copy, weight_copy, sum_copy, *last_copies]:
+    last_copy = pltpu.make_async_remote_copy(
+        src_ref=context_late.at[theirs], dst_ref=last_in, send_sem=last_sem.at[0],
+        recv_sem=last_sem.at[1], device_id=twin, device_id_type=MESH,
+    )
+    last_copy.start()
+    tail[...] = hidden[mine, :] + dot(context_late[mine, :], po_v[...])
+    last_copy.wait_recv()
+    out[...] = (tail[...] + dot(last_in[...], p_other[...])).astype(BF16)
+    for copy in [half_copy, *weight_copies, sum_copy, last_copy]:
         copy.wait_send()
     for slot in range(NEIGH):
         for copy in list_copies(slot):
@@ -379,9 +371,9 @@
         pltpu.VMEM((pairs * 2 * nodes, 2 * LANES), BF16),
         pltpu.VMEM((nodes, width), F32),
         pltpu.VMEM((nodes, cols), BF16),
-        pltpu.VMEM((nodes, width), F32),
-        pltpu.VMEM((STEPS, nodes // 2, width // STEPS), BF16),
-        pltpu.VMEM((STEPS, nodes // 2, width // STEPS), BF16),
+        pltpu.VMEM((nodes // 2, width), F32),
+        pltpu.VMEM((nodes // 2, cols), BF16),
+        pltpu.VMEM((cols, width), BF16),
         pltpu.VMEM((cols, width), BF16),
         pltpu.VMEM((3, cols, cols), BF16),
         pltpu.VMEM((nodes, cols), BF16),
@@ -394,9 +386,11 @@
         pltpu.SemaphoreType.DMA((2 * NEIGH,)),
         pltpu.SemaphoreType.DMA((2 * NEIGH,)),
         pltpu.SemaphoreType.DMA((2,)),
+        pltpu.SemaphoreType.DMA((2,)),
         pltpu.SemaphoreType.DMA((1,)),
         pltpu.SemaphoreType.DMA((1,)),
-    ] + [pltpu.SemaphoreType.DMA((STEPS,))] * 2 + [pltpu.SemaphoreType.REGULAR]
+        pltpu.SemaphoreType.DMA((2,)),
+    ] + [pltpu.SemaphoreType.REGULAR]
     return pl.pallas_call(
         kernel,
         out_shape=pltpu.VMEM((nodes // 2, width), BF16),

time: 24.5 us -> 24.3 us (level)
  Pallas kernels: 23.8 us -> 23.5 us
    pallas_call x1, Pallas kernels: 23.8 us -> 23.5 us  [local(): pl.pallas_call(kernel, out_shape=pltpu.VMEM((nodes // 2, width), BF16), i...]
where the time goes in v6:
time: 24.3 us; the launch traced here: 24.1 us
  Pallas kernels  23.5 us (97%)
  local copies, waits for them, and re-layouts  0.66 us (3%)
    pallas_call x1, Pallas kernels, local(): pl.pallas_call(kernel, out_shape=pltpu.VMEM((nodes // 2, width), BF16), i...  23.5 us
    unnamed x1, local copies, waits for them, and re-layouts  0.66 us

profile of v6, /device:TPU:1, one launch (start us, length us, event | category | flops | bytes accessed | tf_op | source)
XLA Modules:
  0.0 24.1 jit_solution(8560546592941887573)
XLA Ops:
  0.0 23.5 %encode_and_process.1 = bf16[64,1024]{1,0:T(8,128)(2,1)S(1)} custom-call(bf16[100,256]{1,0:T(8,128)(2,1)} %fields.1, bf16[128,1024]{1,0:T(8,128)(2,1)} %mesh_state.1, bf16[100,1024]{1,0:T(8,128)(2,1)} %w_embed.1, bf16[1024,512]{1,0:T(8,128)(2,1)} %w_q.1, bf16[1024,512]{1,0:T(8,128)(2,1)} %w_k.1, bf16[1024,512]{1,0:T(8,128)(2,1)} %w_v.1, ...), custom_call_target="tpu_custom_call" | custom-call | flops 3000000000 | bytes 9500000 | tf_op jit(solution)/shard_map/encode_and_process/pallas_call | solution.py:394
  23.5 0.7 %copy.16 = bf16[64,1024]{1,0:T(8,128)(2,1)} copy(bf16[64,1024]{1,0:T(8,128)(2,1)S(1)} %encode_and_process.1) | data formatting | bytes 262144

commit v7 on v6

--- a/solution.py
+++ b/solution.py
@@ -253,6 +253,8 @@
         logits = dot(queries[rows_of(pair), :], table[...])
         top, probs = weigh(logits, bias[:, 0:points], inverse)
         near.append((join_heads(top), *mix(probs, values[:, lanes_of(pair)])))
+
+    shift = jnp.mean(mesh_v[...].astype(F32), axis=-1, keepdims=True)
 
     loaded(pq_v, pk_v, pv_v, po_v)
     for copy in weight_copies:
@@ -299,9 +301,7 @@
         device_id=twin, device_id_type=MESH,
     )
     sum_copy.start()
-    start = mesh_v[...].astype(F32) + dot(context[...], wo_v[...])
-    shift = jnp.mean(start, axis=-1, keepdims=True)
-    start = start - shift
+    start = mesh_v[...].astype(F32) - shift + dot(context[...], wo_v[...])
     hidden[...] = start
     start = start.astype(BF16)
     for index, weight in enumerate(processor):

time: 24.3 us -> 24.3 us (level)
  no operation moved by 1% of the time
where the time goes in v7:
time: 24.3 us; the launch traced here: 24.2 us
  Pallas kernels  23.5 us (97%)
  local copies, waits for them, and re-layouts  0.66 us (3%)
    pallas_call x1, Pallas kernels, local(): pl.pallas_call(kernel, out_shape=pltpu.VMEM((nodes // 2, width), BF16), i...  23.5 us
    unnamed x1, local copies, waits for them, and re-layouts  0.66 us

profile of v7, /device:TPU:1, one launch (start us, length us, event | category | flops | bytes accessed | tf_op | source)
XLA Modules:
  0.0 24.2 jit_solution(8375700952166599943)
XLA Ops:
  0.0 23.5 %encode_and_process.1 = bf16[64,1024]{1,0:T(8,128)(2,1)S(1)} custom-call(bf16[100,256]{1,0:T(8,128)(2,1)} %fields.1, bf16[128,1024]{1,0:T(8,128)(2,1)} %mesh_state.1, bf16[100,1024]{1,0:T(8,128)(2,1)} %w_embed.1, bf16[1024,512]{1,0:T(8,128)(2,1)} %w_q.1, bf16[1024,512]{1,0:T(8,128)(2,1)} %w_k.1, bf16[1024,512]{1,0:T(8,128)(2,1)} %w_v.1, ...), custom_call_target="tpu_custom_call" | custom-call | flops 3000000000 | bytes 9500000 | tf_op jit(solution)/shard_map/encode_and_process/pallas_call | solution.py:394
  23.5 0.7 %copy.16 = bf16[64,1024]{1,0:T(8,128)(2,1)} copy(bf16[64,1024]{1,0:T(8,128)(2,1)S(1)} %encode_and_process.1) | data formatting | bytes 262144

commit v8 on v7

--- a/solution.py
+++ b/solution.py
@@ -50,7 +50,7 @@
     other_v, listed, received, table, last, values, bias, queries, hidden,     context, tail, last_in, w_other, p_other, w_joint, context_in, ahead_sum,
     context_late,
     load_sem, half_sem, list_send, list_recv, weight_send, weight_recv, sum_send, sum_recv, last_sem,
-    wrap_sem,
+    wrap_sem, late_sem,
 ):
     n = lax.axis_size("nodes")
     region, core = lax.axis_index("nodes"), lax.axis_index("heads")
@@ -86,6 +86,13 @@
     for _, target in pieces[:3]:
         loads[id(target)].start()
     barrier = pltpu.get_barrier_semaphore()
+    edge = n - 2
+    ahead = [slot for slot in range(NEIGH) if offset_of(slot) > 0]
+    behind = [slot for slot in range(NEIGH) if offset_of(slot) < 0]
+    late = sum((region + offset_of(slot) < 0).astype(jnp.int32) for slot in behind)
+    wraps = sum((region + offset_of(slot) >= n).astype(jnp.int32) for slot in ahead)
+    feeds = sum((region - offset_of(slot) < edge).astype(jnp.int32) for slot in ahead)
+    in_last = (region >= edge).astype(jnp.int32)
 
     def greet(slot, semaphore):
         for other in range(2):
@@ -93,13 +100,16 @@
                 semaphore, inc=1, device_id=neighbour(slot, other), device_id_type=MESH
             )
 
-    pl.semaphore_signal(barrier, inc=1, device_id=twin, device_id_type=MESH)
+    @pl.when(region < edge)
+    def _():
+        pl.semaphore_signal(barrier, inc=1, device_id=twin, device_id_type=MESH)
+
     for slot in range(NEIGH):
-        if offset_of(slot) < 0:
-            greet(slot, barrier)
+        place = region + offset_of(slot)
+        if slot in ahead:
+            pl.when(place < edge)(functools.partial(greet, slot, barrier))
         else:
-            pl.when(region + offset_of(slot) < n)(functools.partial(greet, slot, barrier))
-    late = sum((region + offset_of(slot) < 0).astype(jnp.int32) for slot in range(NEIGH))
+            pl.when((region < edge) | (place < edge))(functools.partial(greet, slot, barrier))
     for _, target in pieces[3:]:
         loads[id(target)].start()
 
@@ -111,7 +121,8 @@
     pick = (iota((half, remote), 0) == wanted).astype(BF16)
     listed[...] = dot(own, pick).T.astype(BF16)
 
-    pl.semaphore_wait(barrier, 1 + 2 * NEIGH - 2 * late)
+    pl.semaphore_wait(barrier, (1 - in_last) * (1 + 2 * NEIGH - 2 * late) + in_last * 2 * wraps)
+
     def list_copies(slot):
         part = pl.ds(slot * cap, cap)
         return [
@@ -127,12 +138,17 @@
         for copy in list_copies(slot):
             copy.start()
 
-    ahead = [slot for slot in range(NEIGH) if offset_of(slot) > 0]
-    behind = [slot for slot in range(NEIGH) if offset_of(slot) < 0]
     for slot in ahead:
-        send_list(slot)
+        place = region + offset_of(slot)
+        pl.when((region < edge) | (place >= n))(functools.partial(send_list, slot))
     for slot in ahead:
-        pl.when(region + offset_of(slot) >= n)(functools.partial(greet, slot, wrap_sem))
+        place = region + offset_of(slot)
+        pl.when(place >= n)(functools.partial(greet, slot, wrap_sem))
+        pl.when((region < edge) & (place >= edge))(functools.partial(greet, slot, late_sem))
+    pl.when(region >= edge)(lambda: pl.semaphore_wait(late_sem, 2 * feeds))
+    for slot in ahead:
+        place = region + offset_of(slot)
+        pl.when((region >= edge) & (place < n))(functools.partial(send_list, slot))
     for slot in behind:
         pl.when(region + offset_of(slot) >= 0)(functools.partial(send_list, slot))
     half_copy = pltpu.make_async_remote_copy(
@@ -390,7 +406,7 @@
         pltpu.SemaphoreType.DMA((1,)),
         pltpu.SemaphoreType.DMA((1,)),
         pltpu.SemaphoreType.DMA((2,)),
-    ] + [pltpu.SemaphoreType.REGULAR]
+    ] + [pltpu.SemaphoreType.REGULAR] * 2
     return pl.pallas_call(
         kernel,
         out_shape=pltpu.VMEM((nodes // 2, width), BF16),

time: 24.3 us -> 24.2 us (level)
  no operation moved by 1% of the time
where the time goes in v8:
time: 24.2 us; the launch traced here: 24.1 us
  Pallas kernels  23.4 us (97%)
  local copies, waits for them, and re-layouts  0.66 us (3%)
    pallas_call x1, Pallas kernels, local(): pl.pallas_call(kernel, out_shape=pltpu.VMEM((nodes // 2, width), BF16), i...  23.4 us
    unnamed x1, local copies, waits for them, and re-layouts  0.66 us

profile of v8, /device:TPU:1, one launch (start us, length us, event | category | flops | bytes accessed | tf_op | source)
XLA Modules:
  0.0 24.1 jit_solution(15731974635626912311)
XLA Ops:
  0.0 23.4 %encode_and_process.1 = bf16[64,1024]{1,0:T(8,128)(2,1)S(1)} custom-call(bf16[100,256]{1,0:T(8,128)(2,1)} %fields.1, bf16[128,1024]{1,0:T(8,128)(2,1)} %mesh_state.1, bf16[100,1024]{1,0:T(8,128)(2,1)} %w_embed.1, bf16[1024,512]{1,0:T(8,128)(2,1)} %w_q.1, bf16[1024,512]{1,0:T(8,128)(2,1)} %w_k.1, bf16[1024,512]{1,0:T(8,128)(2,1)} %w_v.1, ...), custom_call_target="tpu_custom_call" | custom-call | flops 3000000000 | bytes 9500000 | tf_op jit(solution)/shard_map/encode_and_process/pallas_call | solution.py:410
  23.4 0.7 %copy.16 = bf16[64,1024]{1,0:T(8,128)(2,1)} copy(bf16[64,1024]{1,0:T(8,128)(2,1)S(1)} %encode_and_process.1) | data formatting | bytes 262144
